TPU v7x, 256 devices: a whole 4x4x8 slice. The times are simulated.
256 devices in a mesh: seq: 16 (over y, x_lo, core), expert: 16 (over z, x_hi).
Axes of the slice: x: 4 (x_hi: 2, x_lo: 2; x = x_hi * 2 + x_lo), y: 4, z: 8, core: 2. Of those that a mesh axis runs over, the one named last changes fastest.
Arguments:
- tokens: bfloat16 [16, 16384, 1280], P('expert', 'seq'), may hold values from -40 to 40
- slot_params: bfloat16 [1280, 128], P(None, 'expert'), may hold values from -6.1 to 6.1
- up_weight: bfloat16 [128, 1280, 2560], P('expert', None, 'seq'), may hold values from -0.625 to 0.625
- down_weight: bfloat16 [128, 2560, 1280], P('expert', 'seq'), may hold values from -0.125 to 0.125
Outputs:
- mixed: bfloat16 [16, 16384, 1280], P('expert', 'seq')
All inputs are finite; a program needn't handle non-finite values.
Results may differ from a plain program's by a relative error of at most 0.0071.
Values may be sent and summed in bfloat16 or wider, within the bound.
A program may use at most 64 MiB of HBM per device.

v0:
```python
import jax
import jax.numpy as jnp
from jax import lax
from jax.sharding import PartitionSpec as P


def shards(tokens, slot_params, up_weight, down_weight):
    clip_dev, patch_dev, width = tokens.shape
    flat_rows = tokens.reshape(clip_dev * patch_dev, width)
    whole_table = lax.all_gather(slot_params, "expert", axis=1, tiled=True)
    logits = jnp.dot(flat_rows, whole_table, preferred_element_type=jnp.float32)
    slots = logits.shape[1]
    logits = logits.reshape(clip_dev, patch_dev, slots)
    local_top = jnp.max(logits, axis=1)
    top = lax.pmax(local_top, "seq")
    scaled = jnp.exp(logits - top[:, None, :])
    totals = jnp.sum(scaled, axis=1)
    weights = scaled.astype(jnp.bfloat16)
    partial_sums = jnp.einsum("cps,cpd->csd", weights, tokens, preferred_element_type=jnp.float32)
    totals, gathered = lax.psum((totals, partial_sums), "seq")
    slot_in = (gathered / totals[:, :, None]).astype(jnp.bfloat16)
    arrived = lax.all_to_all(slot_in, "expert", split_axis=1, concat_axis=0, tiled=True)
    inner = jnp.einsum("ced,edf->cef", arrived, up_weight, preferred_element_type=jnp.float32)
    hidden = jax.nn.gelu(inner, approximate=False).astype(jnp.bfloat16)
    expert_terms = jnp.einsum(
        "cef,efd->ced", hidden, down_weight, preferred_element_type=jnp.float32
    )
    leaving = lax.psum(expert_terms, "seq").astype(jnp.bfloat16)
    returned = lax.all_to_all(leaving, "expert", split_axis=0, concat_axis=1, tiled=True)
    peak = jnp.max(logits, axis=2)
    expo = jnp.exp(logits - peak[:, :, None])
    mix_weights = (expo / jnp.sum(expo, axis=2)[:, :, None]).astype(jnp.bfloat16)
    mixed = jnp.einsum("cps,csd->cpd", mix_weights, returned, preferred_element_type=jnp.float32)
    return mixed.astype(jnp.bfloat16)


def solution(mesh):
    in_specs = (
        P("expert", "seq", None),
        P(None, "expert"),
        P("expert", None, "seq"),
        P("expert", "seq", None),
    )
    out_specs = P("expert", "seq", None)
    return jax.shard_map(shards, mesh=mesh, in_specs=in_specs, out_specs=out_specs, check_vma=False)
```

profile of v0, /device:TPU:1, one launch (start us, length us, event | category | flops | bytes accessed | tf_op | source)
XLA Modules:
  0.0 330.0 jit_solution(7548598207952033417)
XLA Ops:
  6.5 0.0 copy-start
  6.5 0.0 all-reduce.3.cloned.1.call-start
  6.5 39.6 %all_gather.3 = bf16[1280,128]{0,1:T(8,128)(2,1)S(1)} all-gather(bf16[1280,8]{0,1:T(8,128)(2,1)} %param.5), channel_id=1, replica_groups=mesh['seq'=16,'expert'=16] {'expert'}, dimensions={1}, use_global_device_ids=true | all-gather | bytes 348160 | tf_op jit(solution)/shard_map/all_gather | solution.py:10
  46.2 3.4 %fusion.100 = (f32[1024]{0:T(1024)S(1)}, f32[128]{0:T(128)S(1)}, f32[1024,128]{1,0:T(8,128)}) fusion(bf16[1280,128]{0,1:T(8,128)(2,1)S(1)} %all_gather.3, bf16[1,1024,1280]{2,1,0:T(8,128)(2,1)} %param.4), kind=kOutput, calls=%fused_computation.106 | convolution fusion | flops 335805312 | bytes 3478016 | tf_op jit(solution)/shard_map/dot_general | solution.py:11
  49.6 34.3 %pmax.7 = f32[128]{0:T(128)S(1)} all-reduce(f32[128]{0:T(128)S(1)} %get-tuple-element.8), channel_id=1, replica_groups=mesh['seq'=16,'expert'=16] {'seq'}, use_global_device_ids=true, to_apply=%region_3.0 | all-reduce | flops 128 | bytes 1024 | tf_op jit(solution)/shard_map/pmax | solution.py:15
  83.9 3.3 %fusion.5 = f32[1,128,1280]{2,1,0:T(8,128)} fusion(bf16[1,1024,1280]{2,1,0:T(8,128)(2,1)} %param.4, f32[1024,128]{1,0:T(8,128)} %get-tuple-element.9, f32[128]{0:T(128)S(1)} %pmax.7), kind=kOutput, calls=%fused_computation.6 | convolution fusion | flops 335806464 | bytes 3801600 | tf_op jit(solution)/shard_map/cps,cpd->csd/dot_general | solution.py:19
  87.2 0.0 all-reduce.3.cloned.1.call-update
  87.2 1.4 fusion.8
  88.6 27.1 %psum.22 = f32[128]{0:T(128)S(1)} all-reduce(f32[128]{0:T(128)S(1)} %get-tuple-element.6), channel_id=1, replica_groups=mesh['seq'=16,'expert'=16] {'seq'}, use_global_device_ids=true, to_apply=%region_6.0 | all-reduce | flops 128 | bytes 1024 | tf_op jit(solution)/shard_map/psum | solution.py:20
  115.8 87.8 %all-reduce.3.cloned.1.call-done = f32[1,128,1280]{2,1,0:T(8,128)} async-done(((f32[1,128,1280]{2,1,0:T(8,128)}), f32[1,128,1280]{2,1,0:T(8,128)}) %all-reduce.3.cloned.1.call-update) | async-done | bytes 655376 | tf_op jit(solution)/shard_map/psum | solution.py:20
  203.5 1.2 divide_convert_fusion
  204.7 1.3 copy.23
  206.1 0.6 broadcast.21
  206.7 4.3 %reduce.8 = bf16[128,1280]{1,0:T(8,128)(2,1)} reduce(bf16[128,1,1280]{2,1,0:T(2,128)(2,1)} %bitcast.95, bf16[]{:T(256)} %broadcast.21), dimensions={1}, to_apply=%bitcast.94.reduce_sub_computation | reduce | bytes 655362
  210.9 1.8 reshape.51
  212.8 21.9 %all_to_all.21 = bf16[16,2,5120]{2,1,0:T(2,128)(2,1)} all-to-all(bf16[16,2,5120]{2,1,0:T(2,128)(2,1)} %reshape.51), channel_id=1, replica_groups=mesh['seq'=16,'expert'=16] {'expert'}, dimensions={0} | all-to-all | bytes 655360 | tf_op jit(solution)/shard_map/all_to_all | solution.py:22
  234.6 3.2 reshape.52
  237.9 1.8 copy.22
  239.7 0.0 copy-done
  239.7 4.4 %convolution_bitcast_fusion = f32[16,8,1280]{2,0,1:T(8,128)} fusion(bf16[8,160,1280]{2,1,0:T(8,128)(2,1)S(1)} %copy-done, bf16[8,1280,160]{1,2,0:T(8,128)(2,1)} %param.6, bf16[16,8,1280]{2,1,0:T(8,128)(2,1)} %bitcast.97), kind=kOutput, calls=%fused_computation.7 | convolution fusion | flops 106188800 | bytes 7536640 | tf_op jit(solution)/shard_map/cef,efd->ced/dot_general | solution.py:25
  244.1 60.1 %all-reduce.4 = bf16[16,8,1280]{2,0,1:T(8,128)(2,1)} all-reduce(f32[16,8,1280]{2,0,1:T(8,128)} %convolution_bitcast_fusion), channel_id=1, replica_groups=mesh['seq'=16,'expert'=16] {'seq'}, use_global_device_ids=true, to_apply=%region_7.0 | all-reduce | flops 163840 | bytes 983040 | tf_op jit(solution)/shard_map/psum | solution.py:28
  304.1 1.1 copy.12
  305.2 14.4 %all_to_all.22 = bf16[16,8,1280]{2,1,0:T(8,128)(2,1)S(1)} all-to-all(bf16[16,8,1280]{2,1,0:T(8,128)(2,1)S(1)} %copy.12), channel_id=1, replica_groups=mesh['seq'=16,'expert'=16] {'expert'}, dimensions={0} | all-to-all | bytes 655360 | tf_op jit(solution)/shard_map/all_to_all | solution.py:29
  319.6 3.6 %fusion = bf16[1,1024,1280]{2,1,0:T(8,128)(2,1)} fusion(bf16[16,8,1280]{2,1,0:T(8,128)(2,1)S(1)} %all_to_all.22, f32[1024,128]{1,0:T(8,128)} %get-tuple-element.9, f32[1024]{0:T(1024)S(1)} %get-tuple-element.5, f32[1024]{0:T(1024)S(1)} %get-tuple-element.7), kind=kOutput, calls=%fused_computation.1 | convolution fusion | flops 337248256 | bytes 3481600 | tf_op jit(solution)/shard_map/cps,csd->cpd/dot_general | solution.py:33
Async XLA Ops:
  6.5 233.2 %copy-start = (bf16[8,160,1280]{2,1,0:T(8,128)(2,1)S(1)}, bf16[8,160,1280]{2,1,0:T(8,128)(2,1)}, u32[]{:S(2)}) copy-start(bf16[8,160,1280]{2,1,0:T(8,128)(2,1)} %param.7) | copy-start | bytes 9830404
  6.5 197.0 %all-reduce.3.cloned.1.call-start = ((), (), s32[]{:S(2)}) async-start(), calls=%async_computation.2 | async-start | bytes 1310720 | tf_op jit(solution)/shard_map/psum | solution.py:20
Sparse Core Ops, SparseCore 0:
  87.3 116.1 all-reduce.2
where the time goes:
time: 334 us; the launch traced here: 330 us
  blocking collectives  197 us (59%)
  waiting for transfers between devices  87.8 us (26%)
  matrix products  14.6 us (4%)
  between operations  13.4 us (4%)
  local copies, waits for them, and re-layouts  9.88 us (3%)
  other arithmetic  6.89 us (2%)
    psum x1, waiting for transfers between devices, shards(): totals, gathered = lax.psum((totals, partial_sums), 'seq')  87.8 us
    psum x1, blocking collectives, shards(): leaving = lax.psum(expert_terms, 'seq').astype(jnp.bfloat16)  60.1 us
    all_gather x1, blocking collectives, shards(): whole_table = lax.all_gather(slot_params, 'expert', axis=1, tiled=True)  39.6 us
    pmax x1, blocking collectives, shards(): top = lax.pmax(local_top, 'seq')  34.3 us
    psum x1, blocking collectives, shards(): totals, gathered = lax.psum((totals, partial_sums), 'seq')  27.1 us
    all_to_all x1, blocking collectives, shards(): lax.all_to_all(slot_in, 'expert', split_axis=1, concat_axis=0, tiled=True)  21.9 us
    all_to_all x1, blocking collectives, shards(): lax.all_to_all(leaving, 'expert', split_axis=0, concat_axis=1, tiled=True)  14.4 us
    unnamed x6, local copies, waits for them, and re-layouts  7.47 us
  transfers between devices with their start and end apart: 1, of which 1 were waited for; matrix products, arithmetic and copies ran while one was open for 0% of the time, Pallas kernels for 0%

commit v1 on v0

v1 whole, which is shorter than its diff:
```python
import jax
import jax.numpy as jnp
from jax import lax
from jax.experimental import pallas as pl
from jax.experimental.pallas import tpu as pltpu
from jax.sharding import PartitionSpec as P

MESH = pl.DeviceIdType.MESH
BF = jnp.bfloat16
F32 = jnp.float32
NE = 16
NC = 8
K = 8
HALF = 640
ROWS = 1024
FD = 160
SLOTS = NE * K

EXP_ORDER = (7, 9, 8, 5, 11, 6, 10, 3, 13, 4, 12, 1, 15, 2, 14)
EXP_NEAR = tuple(reversed(EXP_ORDER))
CHIP_ORDER = (3, 5, 4, 1, 7, 2, 6)
CHIP_NEAR = (0, 2, 6, 1, 7, 4, 3, 5)


def nt(a, b):
    return lax.dot_general(a, b, (((1,), (1,)), ((), ())), preferred_element_type=F32)


def mm(a, b):
    return jnp.dot(a, b, preferred_element_type=F32)


def gelu(v):
    return 0.5 * v * (1.0 + lax.erf(v * 0.7071067811865476))


def kernel(
    tok_hbm, sp_hbm, up_hbm, dn_hbm, out_ref,
    tokh, upv, dnv, tab, lg, wt, xs, stat, pst, cst, fin, ft,
    psend, pown, precv, rs_send, rs_recv, a_send, a_recv, xb,
    po_send, po_own, po_recv, ro_send, ro_recv, b_send, b_recv, ret, mxs, mw,
    load_sem, tab_s, tab_r, tabf_s, tabf_r, pst_s, pst_r, cst_s, cst_r, pp_s, pp_r,
    rs_s, rs_r, a_s, a_r, xg_s, xg_r, xf_s, xf_r, po_s, po_r, ro_s, ro_r, b_s, b_r,
    rg_s, rg_r, rf_s, rf_r,
):
    s = lax.axis_index("seq")
    e = lax.axis_index("expert")
    chip = lax.div(s, 2)
    h = lax.rem(s, 2)
    o = 1 - h
    sib = (chip * 2 + o, e)

    def chip_at(j):
        return lax.rem(chip + j, NC)

    def chip_dev(j):
        return (chip_at(j) * 2 + h, e)

    def exp_at(i):
        return lax.rem(e + i, NE)

    def copy(src, dst, ssem, rsem, dev):
        return pltpu.make_async_remote_copy(
            src_ref=src, dst_ref=dst, send_sem=ssem, recv_sem=rsem, device_id=dev, device_id_type=MESH
        )

    own = pltpu.make_async_copy(sp_hbm.at[:, pl.ds(0, HALF)], tab.at[0, e], load_sem.at[0])
    own1 = pltpu.make_async_copy(sp_hbm.at[:, pl.ds(HALF, HALF)], tab.at[1, e], load_sem.at[1])
    own.start()
    own1.start()
    loads = []
    for a, (src, dst) in enumerate(((tok_hbm, tokh), (up_hbm, upv), (dn_hbm, dnv))):
        for half in range(2):
            lanes = pl.ds(half * HALF, HALF)
            view = src.at[:, lanes] if a == 0 else src.at[:, :, lanes]
            c = pltpu.make_async_copy(view, dst.at[half], load_sem.at[2 + 2 * a + half])
            c.start()
            loads.append(c)

    barrier = pltpu.get_barrier_semaphore()
    for i in EXP_ORDER:
        pl.semaphore_signal(barrier, inc=1, device_id=(s, exp_at(i)), device_id_type=MESH)
    for j in CHIP_ORDER:
        pl.semaphore_signal(barrier, inc=1, device_id=chip_dev(j), device_id_type=MESH)
    pl.semaphore_signal(barrier, inc=1, device_id=sib, device_id_type=MESH)
    own.wait()
    own1.wait()
    pl.semaphore_wait(barrier, NE - 1 + NC - 1 + 1)

    sends = []
    for i in EXP_ORDER:
        c = copy(tab.at[h, e], tab.at[h, e], tab_s.at[i], tab_r.at[i], (s, exp_at(i)))
        c.start()
        sends.append(c)
    fin[...] = jnp.zeros_like(fin)
    for i in EXP_NEAR:
        src = tab.at[h, exp_at(NE - i)]
        copy(src, src, tab_s.at[i], tab_r.at[i], (s, exp_at(i))).wait_recv()
        c = copy(src, src, tabf_s.at[i], tabf_r.at[i], sib)
        c.start()
        sends.append(c)
    loads[0].wait()
    loads[1].wait()
    half_table = tab[h].astype(F32).reshape(SLOTS, HALF).astype(BF)
    for n in range(4):
        part = pl.ds(n * 256, 256)
        lg[:, part] = nt(half_table, tokh[h, part, :])
    for i in EXP_NEAR:
        src = tab.at[o, exp_at(NE - i)]
        copy(src, src, tabf_s.at[i], tabf_r.at[i], sib).wait_recv()
    half_table = tab[o].astype(F32).reshape(SLOTS, HALF).astype(BF)
    for n in range(4):
        part = pl.ds(n * 256, 256)
        lg[:, part] += nt(half_table, tokh[o, part, :])

    lane = lax.broadcasted_iota(jnp.int32, (32, 128), 1)
    for r in range(0, SLOTS, 32):
        part = pl.ds(r, 32)
        v = lg[part, :]
        m = jnp.max(v, axis=1, keepdims=True)
        ex = jnp.exp(v - m)
        l = jnp.sum(ex, axis=1, keepdims=True)
        wt[part, :] = ex.astype(BF)
        xs[part, :] = jnp.where(lane < 64, m, l)
    xt = xs[...].T
    m0 = jnp.broadcast_to(xt[0:1, :], (8, 128))
    l0 = jnp.broadcast_to(xt[64:65, :], (8, 128))
    stat[0] = m0
    stat[1] = l0
    c_pst = copy(stat, pst, pst_s, pst_r, sib)
    c_pst.start()

    psend[...] = mm(wt[...], tokh[o])
    c_pst.wait_recv()
    m1 = pst[0]
    mc = jnp.maximum(m0, m1)
    g0 = jnp.exp(m0 - mc)
    cst[0, 0] = mc
    cst[0, 1] = l0 * g0 + pst[1] * jnp.exp(m1 - mc)
    c_cst = []
    for j in CHIP_ORDER:
        c = copy(cst.at[0], cst.at[j], cst_s.at[j], cst_r.at[j], chip_dev(j))
        c.start()
        c_cst.append(c)
    scale = jnp.broadcast_to(g0[0:1, :], (128, 128)).T
    for n in range(5):
        part = pl.ds(n * 128, 128)
        psend[:, part] = psend[:, part] * scale
    c_pp = copy(psend, precv, pp_s, pp_r, sib)
    c_pp.start()
    sums = mm(wt[...], tokh[h])
    for n in range(5):
        pown[n] = sums[:, n * 128 : n * 128 + 128] * scale
    c_pp.wait_recv()
    for n in range(5):
        part = pl.ds(n * 128, 128)
        pown[n] = pown[n] + precv[:, part]
        for k in range(K):
            rs_send[k, :, part] = pown[n, pl.ds(k, NE, stride=K), :].astype(BF)
    c_rs = []
    for j in CHIP_ORDER:
        c = copy(rs_send.at[chip_at(j)], rs_recv.at[j], rs_s.at[j], rs_r.at[j], chip_dev(j))
        c.start()
        c_rs.append(c)

    for n in range(4):
        part = pl.ds(n * 256, 256)
        v = lg[:, part]
        ex = jnp.exp(v - jnp.max(v, axis=0, keepdims=True))
        ex = ex / jnp.sum(ex, axis=0, keepdims=True)
        mxs[2 * n] = ex[:, :128]
        mxs[2 * n + 1] = ex[:, 128:]
    for n in range(8):
        part = pl.ds(n * 128, 128)
        rows = [mxs[n, pl.ds(k, NE, stride=K), :] for k in range(K)]
        mw[part, :] = jnp.concatenate(rows, axis=0).T.astype(BF)

    for c in c_cst:
        c.wait_recv()
    top = cst[0, 0]
    for j in range(1, NC):
        top = jnp.maximum(top, cst[j, 0])
    total = jnp.zeros((8, 128), F32)
    for j in range(NC):
        total += cst[j, 1] * jnp.exp(cst[j, 0] - top)
    row = lax.broadcasted_iota(jnp.int32, (8, 128), 0)
    factors = jnp.zeros((8, 128), F32)
    for j in range(NC):
        factors = jnp.where(row == j, jnp.exp(cst[j, 0] - top) / total, factors)
    fin[0:8, :] = factors
    ft[...] = fin[...].T
    fk = ft[pl.ds(chip, NE, stride=K), :]

    y = rs_send[chip].astype(F32) * fk[:, 0:1]
    for c in sends:
        c.wait_send()
    c_pst.wait_send()
    c_pp.wait_send()
    for c in c_cst:
        c.wait_send()
    for j in CHIP_NEAR[1:]:
        copy(rs_recv.at[j], rs_recv.at[j], rs_s.at[j], rs_r.at[j], chip_dev(j)).wait_recv()
        y += rs_recv[j].astype(F32) * fk[:, j : j + 1]

    def rows_across(value, send, recv, ssem, rsem):
        send[...] = value.reshape(NE, 1, HALF)
        started = []
        for i in EXP_ORDER:
            c = copy(send.at[exp_at(i)], recv.at[e], ssem.at[i], rsem.at[i], (s, exp_at(i)))
            c.start()
            started.append(c)
        recv[e] = send[e]
        for i in EXP_NEAR:
            dst = recv.at[exp_at(NE - i)]
            copy(dst, dst, ssem.at[i], rsem.at[i], (s, exp_at(i))).wait_recv()
        return recv[...].reshape(NE, HALF), started

    def spread(value, buf, gs, gr, fs, fr):
        buf[h, chip] = value
        started = []
        for j in CHIP_ORDER:
            c = copy(buf.at[h, chip], buf.at[h, chip], gs.at[j], gr.at[j], chip_dev(j))
            c.start()
            started.append(c)
        c = copy(buf.at[h, chip], buf.at[h, chip], fs.at[0], fr.at[0], sib)
        c.start()
        started.append(c)
        return started

    def forward(j, buf, gs, gr, fs, fr, started):
        src = buf.at[h, chip_at(NC - j)]
        copy(src, src, gs.at[j], gr.at[j], chip_dev(j)).wait_recv()
        c = copy(src, src, fs.at[j], fr.at[j], sib)
        c.start()
        started.append(c)

    def other_half(j, buf, fs, fr):
        src = buf.at[o, chip_at(NC - j)]
        copy(src, src, fs.at[j], fr.at[j], sib).wait_recv()

    x_own, c_a = rows_across(y, a_send, a_recv, a_s, a_r)
    c_xg = spread(x_own.astype(BF), xb, xg_s, xg_r, xf_s, xf_r)
    for c in c_rs:
        c.wait_send()
    for c in c_a:
        c.wait_send()
    for c in loads[2:]:
        c.wait()

    c_po = []
    c_ro = []

    def expert(j):
        k = chip_at(NC - j)
        inner = nt(xb[h, k], upv[h, k])
        other_half(j, xb, xf_s, xf_r)
        inner += nt(xb[o, k], upv[o, k])
        hidden = gelu(inner).astype(BF)
        po_send[j] = mm(hidden, dnv[o, k])
        c = copy(po_send.at[j], po_recv.at[j], po_s.at[j], po_r.at[j], sib)
        c.start()
        c_po.append(c)
        po_own[j] = mm(hidden, dnv[h, k])

    def reduce_on(j):
        copy(po_send.at[j], po_recv.at[j], po_s.at[j], po_r.at[j], sib).wait_recv()
        po_own[j] = po_own[j] + po_recv[j]
        if j:
            ro_send[j] = po_own[j].astype(BF)
            c = copy(ro_send.at[j], ro_recv.at[j], ro_s.at[j], ro_r.at[j], chip_dev(NC - j))
            c.start()
            c_ro.append(c)

    for n in range(1, 3):
        forward(CHIP_NEAR[n], xb, xg_s, xg_r, xf_s, xf_r, c_xg)
    for n in range(NC):
        expert(CHIP_NEAR[n])
        if n + 3 < NC:
            forward(CHIP_NEAR[n + 3], xb, xg_s, xg_r, xf_s, xf_r, c_xg)
        if n:
            reduce_on(CHIP_NEAR[n - 1])
    reduce_on(CHIP_NEAR[NC - 1])
    y = po_own[0]
    for c in c_xg + c_po:
        c.wait_send()
    for j in CHIP_NEAR[1:]:
        copy(ro_recv.at[j], ro_recv.at[j], ro_s.at[j], ro_r.at[j], chip_dev(j)).wait_recv()
        y += ro_recv[j].astype(F32)

    r_own, c_b = rows_across(y, b_send, b_recv, b_s, b_r)
    c_rg = spread(r_own.astype(BF), ret, rg_s, rg_r, rf_s, rf_r)
    for c in c_ro + c_b:
        c.wait_send()
    for j in CHIP_NEAR[1:]:
        forward(j, ret, rg_s, rg_r, rf_s, rf_r, c_rg)

    def mix(half):
        table = ret[half].reshape(SLOTS, HALF)
        lanes = pl.ds(pl.multiple_of(half * HALF, 128), HALF)
        for n in range(4):
            part = pl.ds(n * 256, 256)
            out_ref[part, lanes] = mm(mw[part, :], table).astype(BF)

    mix(h)
    for j in CHIP_NEAR:
        other_half(j, ret, rf_s, rf_r)
    mix(o)
    for c in c_rg:
        c.wait_send()


def shards(tokens, slot_params, up_weight, down_weight):
    vm = pltpu.VMEM
    dma = pltpu.SemaphoreType.DMA
    call = pl.pallas_call(
        kernel,
        out_shape=jax.ShapeDtypeStruct((ROWS, 2 * HALF), BF),
        in_specs=[pl.BlockSpec(memory_space=pl.ANY)] * 4,
        out_specs=pl.BlockSpec(memory_space=pltpu.VMEM),
        scratch_shapes=[
            vm((2, ROWS, HALF), BF),
            vm((2, K, FD, HALF), BF),
            vm((2, K, FD, HALF), BF),
            vm((2, NE, K, HALF), BF),
            vm((SLOTS, ROWS), F32),
            vm((SLOTS, ROWS), BF),
            vm((SLOTS, 128), F32),
            vm((2, 8, 128), F32),
            vm((2, 8, 128), F32),
            vm((NC, 2, 8, 128), F32),
            vm((128, 128), F32),
            vm((128, 128), F32),
            vm((SLOTS, HALF), F32),
            vm((5, SLOTS, 128), F32),
            vm((SLOTS, HALF), F32),
            vm((NC, NE, HALF), BF),
            vm((NC, NE, HALF), BF),
            vm((NE, 1, HALF), F32),
            vm((NE, 1, HALF), F32),
            vm((2, NC, NE, HALF), BF),
            vm((NC, NE, HALF), F32),
            vm((NC, NE, HALF), F32),
            vm((NC, NE, HALF), F32),
            vm((NC, NE, HALF), BF),
            vm((NC, NE, HALF), BF),
            vm((NE, 1, HALF), F32),
            vm((NE, 1, HALF), F32),
            vm((2, NC, NE, HALF), BF),
            vm((8, SLOTS, 128), F32),
            vm((ROWS, SLOTS), BF),
            dma((8,)),
            dma((NE,)), dma((NE,)), dma((NE,)), dma((NE,)),
            dma, dma,
            dma((NC,)), dma((NC,)),
            dma, dma,
            dma((NC,)), dma((NC,)),
            dma((NE,)), dma((NE,)),
            dma((NC,)), dma((NC,)), dma((NC,)), dma((NC,)),
            dma((NC,)), dma((NC,)),
            dma((NC,)), dma((NC,)),
            dma((NE,)), dma((NE,)),
            dma((NC,)), dma((NC,)), dma((NC,)), dma((NC,)),
        ],
        compiler_params=pltpu.CompilerParams(
            collective_id=0, has_side_effects=True, vmem_limit_bytes=48 * 2**20
        ),
        cost_estimate=pl.CostEstimate(flops=1_400_000_000, bytes_accessed=14_000_000, transcendentals=400_000),
        name="soft_moe",
    )
    mixed = call(
        tokens.reshape(ROWS, 2 * HALF),
        slot_params.T,
        jnp.transpose(up_weight, (0, 2, 1)),
        down_weight,
    )
    return mixed.reshape(tokens.shape)


def solution(mesh):
    in_specs = (
        P("expert", "seq", None),
        P(None, "expert"),
        P("expert", None, "seq"),
        P("expert", "seq", None),
    )
    out_specs = P("expert", "seq", None)
    return jax.shard_map(shards, mesh=mesh, in_specs=in_specs, out_specs=out_specs, check_vma=False)
```

time: 334 us -> 65.4 us (0.20); the launches traced: 330 us -> 65.2 us
  blocking collectives: 197 us -> 0 us
  waiting for transfers between devices: 87.8 us -> 0 us
  Pallas kernels: 0 us -> 61.2 us
  matrix products: 14.6 us -> 0 us
  between operations: 13.4 us -> 0.01 us
  other arithmetic: 6.89 us -> 0 us
  local copies, waits for them, and re-layouts: 9.88 us -> 3.96 us
    psum x1 -> x0, waiting for transfers between devices: 87.8 us -> none  [shards(): totals, gathered = lax.psum((totals, partial_sums), 'seq')]
    psum x2 -> x0, blocking collectives: 87.2 us -> none  [the longest x1 60.1 us: shards(): leaving = lax.psum(expert_terms, 'seq').astype(jnp.bfloat16)]
    pallas_call x0 -> x1, Pallas kernels: none -> 61.2 us  [shards(): call(tokens.reshape(ROWS, 2 * HALF), slot_params.T, jnp.transpose(up_weig...]
    all_gather x1 -> x0, blocking collectives: 39.6 us -> none  [shards(): whole_table = lax.all_gather(slot_params, 'expert', axis=1, tiled=True)]
    all_to_all x2 -> x0, blocking collectives: 36.3 us -> none  [the longest x1 21.9 us: shards(): lax.all_to_all(slot_in, 'expert', split_axis=1, concat_axis=0, tiled=True)]
    pmax x1 -> x0, blocking collectives: 34.3 us -> none  [shards(): top = lax.pmax(local_top, 'seq')]
    dot_general x4 -> x0, matrix products: 14.6 us -> none  [the longest x1 4.37 us: shards(): jnp.einsum('cef,efd->ced', hidden, down_weight, preferred_element_type=jn...]
    unnamed x1 -> x0, other arithmetic: 4.29 us -> none
  transfers between devices with their start and end apart: 1 -> 0, of which waited for: 1 -> 0; matrix products, arithmetic and copies ran while one was open for 0% -> 0% of each run, Pallas kernels for 0% -> 0%
where the time goes in v1:
time: 65.4 us; the launch traced here: 65.2 us
  Pallas kernels  61.2 us (94%)
  local copies, waits for them, and re-layouts  3.96 us (6%)
    pallas_call x1, Pallas kernels, shards(): call(tokens.reshape(ROWS, 2 * HALF), slot_params.T, jnp.transpose(up_weig...  61.2 us
    unnamed x5, local copies, waits for them, and re-layouts  3.96 us

profile of v1, /device:TPU:1, one launch (start us, length us, event | category | flops | bytes accessed | tf_op | source)
XLA Modules:
  0.0 65.2 jit_solution(7256881090271291640)
XLA Ops:
  0.0 0.0 copy-start
  0.0 1.7 %copy-done = bf16[1,1024,1280]{2,1,0:T(8,128)(2,1)S(1)} copy-done((bf16[1,1024,1280]{2,1,0:T(8,128)(2,1)S(1)}, bf16[1,1024,1280]{2,1,0:T(8,128)(2,1)}, u32[]{:S(2)}) %copy-start) | copy-done | bytes 2621464
  1.7 0.0 copy-start.1
  1.7 0.7 %copy-done.1 = bf16[1280,8]{0,1:T(8,128)(2,1)S(1)} copy-done((bf16[1280,8]{0,1:T(8,128)(2,1)S(1)}, bf16[1280,8]{0,1:T(8,128)(2,1)}, u32[]{:S(2)}) %copy-start.1) | copy-done | bytes 20504
  2.5 61.2 %soft_moe.1 = bf16[1024,1280]{1,0:T(8,128)(2,1)S(1)} custom-call(bf16[1024,1280]{1,0:T(8,128)(2,1)S(1)} %bitcast.5, bf16[8,1280]{1,0:T(8,128)(2,1)S(1)} %bitcast.6, bf16[8,160,1280]{2,1,0:T(8,128)(2,1)} %bitcast.7, bf16[8,160,1280]{2,1,0:T(8,128)(2,1)} %dn_hbm.1), custom_call_target="tpu_custom_call" | custom-call | flops 1400000000 | bytes 14000000 | tf_op jit(solution)/shard_map/soft_moe/pallas_call | solution.py:370
  63.7 1.5 %copy.6 = bf16[1,1024,1280]{2,1,0:T(8,128)(2,1)} copy(bf16[1,1024,1280]{2,1,0:T(8,128)(2,1)S(1)} %bitcast.4) | data formatting | bytes 5242880
Async XLA Ops:
  0.0 1.7 %copy-start = (bf16[1,1024,1280]{2,1,0:T(8,128)(2,1)S(1)}, bf16[1,1024,1280]{2,1,0:T(8,128)(2,1)}, u32[]{:S(2)}) copy-start(bf16[1,1024,1280]{2,1,0:T(8,128)(2,1)} %param.4) | copy-start | bytes 7864324
  1.7 0.7 %copy-start.1 = (bf16[1280,8]{0,1:T(8,128)(2,1)S(1)}, bf16[1280,8]{0,1:T(8,128)(2,1)}, u32[]{:S(2)}) copy-start(bf16[1280,8]{0,1:T(8,128)(2,1)} %param.5) | copy-start | bytes 61444

commit v2 on v1

v2 whole, which is shorter than its diff:
```python
import jax
import jax.numpy as jnp
from jax import lax
from jax.experimental import pallas as pl
from jax.experimental.pallas import tpu as pltpu
from jax.sharding import PartitionSpec as P

MESH = pl.DeviceIdType.MESH
BF = jnp.bfloat16
F32 = jnp.float32
NE = 16
NZ = 8
NC = 8
K = 8
HALF = 640
ROWS = 1024
FD = 160
SLOTS = NE * K

EXP_FAR = (
    (1, 4), (1, 3), (1, 5), (0, 4), (1, 2), (1, 6), (0, 3), (0, 5),
    (1, 1), (1, 7), (0, 2), (0, 6), (1, 0), (0, 1), (0, 7),
)
EXP_NEAR = tuple(reversed(EXP_FAR))
CHIP_FAR = ((2, 1), (2, 0), (1, 1), (3, 1), (1, 0), (3, 0), (0, 1))
CHIP_NEAR = tuple(reversed(CHIP_FAR))


def nt(a, b):
    return lax.dot_general(a, b, (((1,), (1,)), ((), ())), preferred_element_type=F32)


def mm(a, b):
    return jnp.dot(a, b, preferred_element_type=F32)


def gelu(v):
    return 0.5 * v * (1.0 + lax.erf(v * 0.7071067811865476))


def kernel(
    tok_hbm, sp_hbm, up_hbm, dn_hbm, out_ref,
    tokh, upv, dnv, tab, lg, wt, xs, stat, pst, cst, fin, ft,
    psend, pown, precv, rs_send, rs_recv, a_send, a_recv, xb,
    po_send, po_own, po_recv, ro_send, ro_recv, b_send, b_recv, ret, mxs, mw,
    load_sem, tab_s, tab_r, tabf_s, tabf_r, pst_s, pst_r, cst_s, cst_r, pp_s, pp_r,
    rs_s, rs_r, a_s, a_r, xg_s, xg_r, xf_s, xf_r, po_s, po_r, ro_s, ro_r, b_s, b_r,
    rg_s, rg_r, rf_s, rf_r,
):
    s = lax.axis_index("seq")
    e = lax.axis_index("expert")
    chip = lax.div(s, 2)
    h = lax.rem(s, 2)
    o = 1 - h
    y = lax.div(chip, 2)
    x_lo = lax.rem(chip, 2)
    z = lax.div(e, 2)
    x_hi = lax.rem(e, 2)
    sib = (chip * 2 + o, e)
    flipped = y * 2 + 1 - x_lo

    def chip_at(p):
        return lax.rem(y + p[0], 4) * 2 + (1 - x_lo if p[1] else x_lo)

    def chip_from(p):
        return chip_at((4 - p[0], p[1]))

    def chip_dev(p):
        return (chip_at(p) * 2 + h, e)

    def exp_at(i):
        return lax.rem(z + i[1], NZ) * 2 + (1 - x_hi if i[0] else x_hi)

    def exp_from(i):
        return exp_at((i[0], NZ - i[1]))

    def exp_dev(i):
        return ((flipped if i[0] else chip) * 2 + h, exp_at(i))

    def cid(p):
        return p[0] * 2 + p[1]

    def eid(i):
        return i[0] * NZ + i[1]

    live = []

    def drain(count=None):
        for c in live[:count]:
            c.wait_send()
        del live[:count]

    def copy(src, dst, ssem, rsem, dev):
        return pltpu.make_async_remote_copy(
            src_ref=src, dst_ref=dst, send_sem=ssem, recv_sem=rsem, device_id=dev, device_id_type=MESH
        )

    def send(src, dst, ssem, rsem, dev):
        c = copy(src, dst, ssem, rsem, dev)
        c.start()
        live.append(c)

    def arrived(dst, ssem, rsem):
        copy(dst, dst, ssem, rsem, sib).wait_recv()

    barrier = pltpu.get_barrier_semaphore()
    for i in EXP_FAR:
        pl.semaphore_signal(barrier, inc=1, device_id=exp_dev(i), device_id_type=MESH)
    for p in CHIP_FAR:
        pl.semaphore_signal(barrier, inc=1, device_id=chip_dev(p), device_id_type=MESH)
    pl.semaphore_signal(barrier, inc=1, device_id=sib, device_id_type=MESH)

    loads = []
    for half in range(2):
        lanes = pl.ds(half * HALF, HALF)
        c = pltpu.make_async_copy(sp_hbm.at[:, lanes], tab.at[half, e], load_sem.at[6 + half])
        c.start()
        loads.append(c)
    for a, (src, dst) in enumerate(((tok_hbm, tokh), (up_hbm, upv), (dn_hbm, dnv))):
        for half in range(2):
            lanes = pl.ds(half * HALF, HALF)
            view = src.at[:, lanes] if a == 0 else src.at[:, :, lanes]
            c = pltpu.make_async_copy(view, dst.at[half], load_sem.at[2 * a + half])
            c.start()
            loads.append(c)
    fin[...] = jnp.zeros_like(fin)
    loads[0].wait()
    loads[1].wait()
    pl.semaphore_wait(barrier, NE - 1 + NC - 1 + 1)

    for i in EXP_FAR:
        send(tab.at[h, e], tab.at[h, e], tab_s.at[eid(i)], tab_r.at[eid(i)], exp_dev(i))
    for i in EXP_NEAR:
        src = tab.at[h, exp_from(i)]
        arrived(src, tab_s.at[eid(i)], tab_r.at[eid(i)])
        send(src, src, tabf_s.at[eid(i)], tabf_r.at[eid(i)], sib)
    loads[2].wait()
    loads[3].wait()
    half_table = tab[h].astype(F32).reshape(SLOTS, HALF).astype(BF)
    for n in range(4):
        part = pl.ds(n * 256, 256)
        lg[:, part] = nt(half_table, tokh[h, part, :])
    for i in EXP_NEAR:
        arrived(tab.at[o, exp_from(i)], tabf_s.at[eid(i)], tabf_r.at[eid(i)])
    half_table = tab[o].astype(F32).reshape(SLOTS, HALF).astype(BF)
    for n in range(4):
        part = pl.ds(n * 256, 256)
        lg[:, part] += nt(half_table, tokh[o, part, :])

    lane = lax.broadcasted_iota(jnp.int32, (32, 128), 1)
    for r in range(0, SLOTS, 32):
        part = pl.ds(r, 32)
        v = lg[part, :]
        m = jnp.max(v, axis=1, keepdims=True)
        ex = jnp.exp(v - m)
        l = jnp.sum(ex, axis=1, keepdims=True)
        wt[part, :] = ex.astype(BF)
        xs[part, :] = jnp.where(lane < 64, m, l)
    xt = xs[...].T
    m0 = jnp.broadcast_to(xt[0:1, :], (8, 128))
    l0 = jnp.broadcast_to(xt[64:65, :], (8, 128))
    stat[0] = m0
    stat[1] = l0
    send(stat, pst, pst_s, pst_r, sib)

    for n, w in ((0, 2), (2, 2), (4, 1)):
        sums = mm(wt[...], tokh[o, :, pl.ds(n * 128, w * 128)])
        for q in range(w):
            psend[n + q] = sums[:, q * 128 : q * 128 + 128]
        part = pl.ds(n, w)
        send(psend.at[part], precv.at[part], pp_s.at[n], pp_r.at[n], sib)
    sums = mm(wt[...], tokh[h])
    for n in range(5):
        pown[n] = sums[:, n * 128 : n * 128 + 128]
    arrived(pst, pst_s, pst_r)
    m1 = pst[0]
    mc = jnp.maximum(m0, m1)
    g0 = jnp.exp(m0 - mc)
    g1 = jnp.exp(m1 - mc)
    cst[0, 0] = mc
    cst[0, 1] = l0 * g0 + pst[1] * g1
    for p in CHIP_FAR:
        send(cst.at[0], cst.at[cid(p)], cst_s.at[cid(p)], cst_r.at[cid(p)], chip_dev(p))
    scale0 = jnp.broadcast_to(g0[0:1, :], (128, 128)).T
    scale1 = jnp.broadcast_to(g1[0:1, :], (128, 128)).T

    def unit(ref, k):
        near = ref[pl.ds(8 * x_hi + k, NZ, stride=16), :]
        far = ref[pl.ds(8 * (1 - x_hi) + k + 1 - 2 * lax.rem(k, 2), NZ, stride=16), :]
        return jnp.concatenate([near, far], axis=0)

    for n, w in ((0, 2), (2, 2), (4, 1)):
        arrived(precv.at[pl.ds(n, w)], pp_s.at[n], pp_r.at[n])
        for q in range(n, n + w):
            pown[q] = pown[q] * scale0 + precv[q] * scale1
    older = len(live)
    for p in CHIP_FAR:
        for n in range(5):
            rs_send[cid(p), :, pl.ds(n * 128, 128)] = unit(pown.at[n], chip_at(p)).astype(BF)
        send(rs_send.at[cid(p)], rs_recv.at[cid(p)], rs_s.at[cid(p)], rs_r.at[cid(p)], chip_dev(p))
    yown = jnp.concatenate([unit(pown.at[n], chip) for n in range(5)], axis=1)

    for n in range(4):
        part = pl.ds(n * 256, 256)
        v = lg[:, part]
        ex = jnp.exp(v - jnp.max(v, axis=0, keepdims=True))
        ex = ex / jnp.sum(ex, axis=0, keepdims=True)
        mxs[2 * n] = ex[:, :128]
        mxs[2 * n + 1] = ex[:, 128:]
    for n in range(8):
        part = pl.ds(n * 128, 128)
        rows = []
        for k in range(K):
            rows.append(mxs[n, pl.ds(8 * x_hi + k, NZ, stride=16), :])
            rows.append(mxs[n, pl.ds(8 * (1 - x_hi) + k, NZ, stride=16), :])
        mw[part, :] = jnp.concatenate(rows, axis=0).T.astype(BF)

    drain(older)

    for p in CHIP_NEAR:
        arrived(cst.at[cid(p)], cst_s.at[cid(p)], cst_r.at[cid(p)])
    top = cst[0, 0]
    for j in range(1, NC):
        top = jnp.maximum(top, cst[j, 0])
    total = jnp.zeros((8, 128), F32)
    for j in range(NC):
        total += cst[j, 1] * jnp.exp(cst[j, 0] - top)
    row = lax.broadcasted_iota(jnp.int32, (8, 128), 0)
    factors = jnp.zeros((8, 128), F32)
    for j in range(NC):
        factors = jnp.where(row == j, jnp.exp(cst[j, 0] - top) / total, factors)
    fin[0:8, :] = factors
    ft[...] = fin[...].T
    fk = unit(ft, chip)

    acc = yown * fk[:, 0:1]
    for p in CHIP_NEAR:
        j = cid(p)
        arrived(rs_recv.at[j], rs_s.at[j], rs_r.at[j])
        acc += rs_recv[j].astype(F32) * fk[:, j : j + 1]

    def rows_across(value, rows, recv, ssem, rsem):
        older = len(live)
        rows[...] = value.reshape(NE, 1, HALF)
        for i in EXP_FAR:
            src = rows.at[i[0] * NZ + lax.rem(z + i[1], NZ)]
            send(src, recv.at[i[0] * NZ + z], ssem.at[eid(i)], rsem.at[eid(i)], exp_dev(i))
        recv[z] = rows[z]
        drain(older)
        for i in EXP_NEAR:
            dst = recv.at[i[0] * NZ + lax.rem(z + NZ - i[1], NZ)]
            arrived(dst, ssem.at[eid(i)], rsem.at[eid(i)])
        return recv[...].reshape(NE, HALF)

    def spread(value, buf, gs, gr):
        older = len(live)
        buf[h, chip] = value
        for p in CHIP_FAR:
            send(buf.at[h, chip], buf.at[h, chip], gs.at[cid(p)], gr.at[cid(p)], chip_dev(p))
        drain(older)

    def forward(q, buf, gs, gr, fs, fr):
        for p in ((q, 1), (q, 0)) if q else ((q, 1),):
            arrived(buf.at[h, chip_from(p)], gs.at[cid(p)], gr.at[cid(p)])
        src = buf.at[h, pl.ds(lax.rem(y + 4 - q, 4) * 2, 2)]
        send(src, src, fs.at[q], fr.at[q], sib)

    def other_half(q, buf, fs, fr):
        arrived(buf.at[o, pl.ds(lax.rem(y + 4 - q, 4) * 2, 2)], fs.at[q], fr.at[q])

    across = rows_across(acc, a_send, a_recv, a_s, a_r)
    spread(across.astype(BF), xb, xg_s, xg_r)
    for c in loads[4:]:
        c.wait()

    def experts(q):
        ks = (chip_from((q, 0)), chip_from((q, 1)))
        other_half(q, xb, xf_s, xf_r)
        inner = [nt(xb[0, k], upv[0, k]) + nt(xb[1, k], upv[1, k]) for k in ks]
        hidden = [gelu(v).astype(BF) for v in inner]
        away = [mm(v, dnv[o, k]) for v, k in zip(hidden, ks)]
        for n in range(2):
            po_send[q, n] = away[n]
        send(po_send.at[q], po_recv.at[q], po_s.at[q], po_r.at[q], sib)
        here = [mm(v, dnv[h, k]) for v, k in zip(hidden, ks)]
        for n in range(2):
            po_own[q, n] = here[n]

    def reduce_on(q):
        arrived(po_recv.at[q], po_s.at[q], po_r.at[q])
        both = [po_own[q, n] + po_recv[q, n] for n in range(2)]
        for n in range(2):
            value = jnp.concatenate([both[n][:NZ], both[1 - n][NZ:]], axis=0)
            if q or n:
                ro_send[q, n] = value.astype(BF)
                p = (4 - q if q else 0, n)
                sems = ro_s.at[cid(p)], ro_r.at[cid(p)]
                send(ro_send.at[q, n], ro_recv.at[cid(p)], *sems, chip_dev(p))
            else:
                po_own[0, 0] = value

    forward(0, xb, xg_s, xg_r, xf_s, xf_r)
    forward(1, xb, xg_s, xg_r, xf_s, xf_r)
    forward(3, xb, xg_s, xg_r, xf_s, xf_r)
    experts(0)
    experts(1)
    forward(2, xb, xg_s, xg_r, xf_s, xf_r)
    reduce_on(0)
    experts(3)
    reduce_on(1)
    experts(2)
    older = len(live)
    reduce_on(3)
    reduce_on(2)
    acc = po_own[0, 0]
    drain(older)
    for p in CHIP_NEAR:
        arrived(ro_recv.at[cid(p)], ro_s.at[cid(p)], ro_r.at[cid(p)])
        acc += ro_recv[cid(p)].astype(F32)

    across = rows_across(acc, b_send, b_recv, b_s, b_r)
    spread(across.astype(BF), ret, rg_s, rg_r)
    for q in (0, 1, 3, 2):
        forward(q, ret, rg_s, rg_r, rf_s, rf_r)

    def mix(half):
        table = ret[half].reshape(SLOTS, HALF)
        lanes = pl.ds(pl.multiple_of(half * HALF, 128), HALF)
        for n in range(4):
            part = pl.ds(n * 256, 256)
            out_ref[part, lanes] = mm(mw[part, :], table).astype(BF)

    mix(h)
    for q in (0, 1, 3, 2):
        other_half(q, ret, rf_s, rf_r)
    mix(o)
    drain()


def shards(tokens, slot_params, up_weight, down_weight):
    vm = pltpu.VMEM
    dma = pltpu.SemaphoreType.DMA
    call = pl.pallas_call(
        kernel,
        out_shape=jax.ShapeDtypeStruct((ROWS, 2 * HALF), BF),
        in_specs=[pl.BlockSpec(memory_space=pltpu.HBM)] * 4,
        out_specs=pl.BlockSpec(memory_space=pltpu.VMEM),
        scratch_shapes=[
            vm((2, ROWS, HALF), BF),
            vm((2, K, FD, HALF), BF),
            vm((2, K, FD, HALF), BF),
            vm((2, NE, K, HALF), BF),
            vm((SLOTS, ROWS), F32),
            vm((SLOTS, ROWS), BF),
            vm((SLOTS, 128), F32),
            vm((2, 8, 128), F32),
            vm((2, 8, 128), F32),
            vm((NC, 2, 8, 128), F32),
            vm((128, 128), F32),
            vm((128, 128), F32),
            vm((5, SLOTS, 128), F32),
            vm((5, SLOTS, 128), F32),
            vm((5, SLOTS, 128), F32),
            vm((NC, NE, HALF), BF),
            vm((NC, NE, HALF), BF),
            vm((NE, 1, HALF), F32),
            vm((NE, 1, HALF), F32),
            vm((2, NC, NE, HALF), BF),
            vm((4, 2, NE, HALF), F32),
            vm((4, 2, NE, HALF), F32),
            vm((4, 2, NE, HALF), F32),
            vm((4, 2, NE, HALF), BF),
            vm((NC, NE, HALF), BF),
            vm((NE, 1, HALF), F32),
            vm((NE, 1, HALF), F32),
            vm((2, NC, NE, HALF), BF),
            vm((8, SLOTS, 128), F32),
            vm((ROWS, SLOTS), BF),
            dma((8,)),
            dma((NE,)), dma((NE,)), dma((NE,)), dma((NE,)),
            dma, dma,
            dma((NC,)), dma((NC,)),
            dma((5,)), dma((5,)),
            dma((NC,)), dma((NC,)),
            dma((NE,)), dma((NE,)),
            dma((NC,)), dma((NC,)), dma((4,)), dma((4,)),
            dma((4,)), dma((4,)),
            dma((NC,)), dma((NC,)),
            dma((NE,)), dma((NE,)),
            dma((NC,)), dma((NC,)), dma((4,)), dma((4,)),
        ],
        compiler_params=pltpu.CompilerParams(
            collective_id=0, has_side_effects=True, vmem_limit_bytes=50 * 2**20
        ),
        cost_estimate=pl.CostEstimate(flops=1_400_000_000, bytes_accessed=14_000_000, transcendentals=400_000),
        name="soft_moe",
    )
    mixed = call(
        tokens.reshape(ROWS, 2 * HALF),
        slot_params.T,
        jnp.transpose(up_weight, (0, 2, 1)),
        down_weight,
    )
    return mixed.reshape(tokens.shape)


def solution(mesh):
    in_specs = (
        P("expert", "seq", None),
        P(None, "expert"),
        P("expert", None, "seq"),
        P("expert", "seq", None),
    )
    out_specs = P("expert", "seq", None)
    return jax.shard_map(shards, mesh=mesh, in_specs=in_specs, out_specs=out_specs, check_vma=False)
```

time: 65.4 us -> 59.1 us (0.904)
  Pallas kernels: 61.2 us -> 56.7 us
  local copies, waits for them, and re-layouts: 3.96 us -> 2.22 us
    pallas_call x1, Pallas kernels: 61.2 us -> 56.7 us  [shards(): call(tokens.reshape(ROWS, 2 * HALF), slot_params.T, jnp.transpose(up_weig...]
    unnamed x5 -> x3, local copies, waits for them, and re-layouts: 3.96 us -> 2.22 us
where the time goes in v2:
time: 59.1 us; the launch traced here: 59 us
  Pallas kernels  56.7 us (96%)
  local copies, waits for them, and re-layouts  2.22 us (4%)
    pallas_call x1, Pallas kernels, shards(): call(tokens.reshape(ROWS, 2 * HALF), slot_params.T, jnp.transpose(up_weig...  56.7 us
    unnamed x3, local copies, waits for them, and re-layouts  2.22 us

profile of v2, /device:TPU:1, one launch (start us, length us, event | category | flops | bytes accessed | tf_op | source)
XLA Modules:
  0.0 59.0 jit_solution(1058300652326125555)
XLA Ops:
  0.0 0.0 copy-start
  0.0 0.7 %copy-done = bf16[1280,8]{0,1:T(8,128)(2,1)S(1)} copy-done((bf16[1280,8]{0,1:T(8,128)(2,1)S(1)}, bf16[1280,8]{0,1:T(8,128)(2,1)}, u32[]{:S(2)}) %copy-start) | copy-done | bytes 20504
  0.7 56.7 %soft_moe.1 = bf16[1024,1280]{1,0:T(8,128)(2,1)S(1)} custom-call(bf16[1024,1280]{1,0:T(8,128)(2,1)} %bitcast.7, bf16[8,1280]{1,0:T(8,128)(2,1)S(1)} %bitcast.5, bf16[8,160,1280]{2,1,0:T(8,128)(2,1)} %bitcast.6, bf16[8,160,1280]{2,1,0:T(8,128)(2,1)} %dn_hbm.1), custom_call_target="tpu_custom_call" | custom-call | flops 1400000000 | bytes 14000000 | tf_op jit(solution)/shard_map/soft_moe/pallas_call | solution.py:398
  57.5 1.5 %copy.6 = bf16[1,1024,1280]{2,1,0:T(8,128)(2,1)} copy(bf16[1,1024,1280]{2,1,0:T(8,128)(2,1)S(1)} %bitcast.4) | data formatting | bytes 5242880
Async XLA Ops:
  0.0 0.7 %copy-start = (bf16[1280,8]{0,1:T(8,128)(2,1)S(1)}, bf16[1280,8]{0,1:T(8,128)(2,1)}, u32[]{:S(2)}) copy-start(bf16[1280,8]{0,1:T(8,128)(2,1)} %param.5) | copy-start | bytes 61444

commit v3 on v2

--- a/solution.py
+++ b/solution.py
@@ -42,9 +42,9 @@
     tok_hbm, sp_hbm, up_hbm, dn_hbm, out_ref,
     tokh, upv, dnv, tab, lg, wt, xs, stat, pst, cst, fin, ft,
     psend, pown, precv, rs_send, rs_recv, a_send, a_recv, xb,
-    po_send, po_own, po_recv, ro_send, ro_recv, b_send, b_recv, ret, mxs, mw,
+    px_send, px_recv, ro_send, ro_own, ro_recv, b_send, b_recv, ret, mxs, mw,
     load_sem, tab_s, tab_r, tabf_s, tabf_r, pst_s, pst_r, cst_s, cst_r, pp_s, pp_r,
-    rs_s, rs_r, a_s, a_r, xg_s, xg_r, xf_s, xf_r, po_s, po_r, ro_s, ro_r, b_s, b_r,
+    rs_s, rs_r, w_s, w_r, a_s, a_r, xg_s, xg_r, px_s, px_r, ro_s, ro_r, b_s, b_r,
     rg_s, rg_r, rf_s, rf_r,
 ):
     s = lax.axis_index("seq")
@@ -85,20 +85,21 @@
 
     live = []
 
-    def drain(count=None):
-        for c in live[:count]:
-            c.wait_send()
-        del live[:count]
+    def drain(groups=None):
+        for item in list(live):
+            if groups is None or item[0] in groups:
+                item[1].wait_send()
+                live.remove(item)
 
     def copy(src, dst, ssem, rsem, dev):
         return pltpu.make_async_remote_copy(
             src_ref=src, dst_ref=dst, send_sem=ssem, recv_sem=rsem, device_id=dev, device_id_type=MESH
         )
 
-    def send(src, dst, ssem, rsem, dev):
+    def send(group, src, dst, ssem, rsem, dev):
         c = copy(src, dst, ssem, rsem, dev)
         c.start()
-        live.append(c)
+        live.append((group, c))
 
     def arrived(dst, ssem, rsem):
         copy(dst, dst, ssem, rsem, sib).wait_recv()
@@ -108,32 +109,39 @@
         pl.semaphore_signal(barrier, inc=1, device_id=exp_dev(i), device_id_type=MESH)
     for p in CHIP_FAR:
         pl.semaphore_signal(barrier, inc=1, device_id=chip_dev(p), device_id_type=MESH)
+    for p in CHIP_FAR:
+        pl.semaphore_signal(barrier, inc=1, device_id=(chip_at(p) * 2 + o, e), device_id_type=MESH)
     pl.semaphore_signal(barrier, inc=1, device_id=sib, device_id_type=MESH)
 
     loads = []
     for half in range(2):
         lanes = pl.ds(half * HALF, HALF)
-        c = pltpu.make_async_copy(sp_hbm.at[:, lanes], tab.at[half, e], load_sem.at[6 + half])
+        c = pltpu.make_async_copy(sp_hbm.at[:, lanes], tab.at[half, e], load_sem.at[4 + half])
         c.start()
         loads.append(c)
-    for a, (src, dst) in enumerate(((tok_hbm, tokh), (up_hbm, upv), (dn_hbm, dnv))):
-        for half in range(2):
-            lanes = pl.ds(half * HALF, HALF)
-            view = src.at[:, lanes] if a == 0 else src.at[:, :, lanes]
-            c = pltpu.make_async_copy(view, dst.at[half], load_sem.at[2 * a + half])
-            c.start()
-            loads.append(c)
+    for half in range(2):
+        c = pltpu.make_async_copy(tok_hbm.at[:, pl.ds(half * HALF, HALF)], tokh.at[half], load_sem.at[half])
+        c.start()
+        loads.append(c)
+    ours = pl.ds(pl.multiple_of(h * HALF, 128), HALF)
+    units = pl.ds(pl.multiple_of(h * FD, 16), FD)
+    their_units = pl.ds(pl.multiple_of(o * FD, 16), FD)
+    for n, (src, dst) in enumerate(((up_hbm, upv), (dn_hbm, dnv))):
+        c = pltpu.make_async_copy(src.at[:, :, ours], dst.at[:, units], load_sem.at[2 + n])
+        c.start()
+        loads.append(c)
     fin[...] = jnp.zeros_like(fin)
+    px_send[...] = jnp.zeros_like(px_send)
     loads[0].wait()
     loads[1].wait()
-    pl.semaphore_wait(barrier, NE - 1 + NC - 1 + 1)
+    pl.semaphore_wait(barrier, NE - 1 + 2 * (NC - 1) + 1)
 
     for i in EXP_FAR:
-        send(tab.at[h, e], tab.at[h, e], tab_s.at[eid(i)], tab_r.at[eid(i)], exp_dev(i))
+        send("tab", tab.at[h, e], tab.at[h, e], tab_s.at[eid(i)], tab_r.at[eid(i)], exp_dev(i))
     for i in EXP_NEAR:
         src = tab.at[h, exp_from(i)]
         arrived(src, tab_s.at[eid(i)], tab_r.at[eid(i)])
-        send(src, src, tabf_s.at[eid(i)], tabf_r.at[eid(i)], sib)
+        send("tab", src, src, tabf_s.at[eid(i)], tabf_r.at[eid(i)], sib)
     loads[2].wait()
     loads[3].wait()
     half_table = tab[h].astype(F32).reshape(SLOTS, HALF).astype(BF)
@@ -161,14 +169,14 @@
     l0 = jnp.broadcast_to(xt[64:65, :], (8, 128))
     stat[0] = m0
     stat[1] = l0
-    send(stat, pst, pst_s, pst_r, sib)
+    send("tab", stat, pst, pst_s, pst_r, sib)
 
     for n, w in ((0, 2), (2, 2), (4, 1)):
         sums = mm(wt[...], tokh[o, :, pl.ds(n * 128, w * 128)])
         for q in range(w):
             psend[n + q] = sums[:, q * 128 : q * 128 + 128]
         part = pl.ds(n, w)
-        send(psend.at[part], precv.at[part], pp_s.at[n], pp_r.at[n], sib)
+        send("pp", psend.at[part], precv.at[part], pp_s.at[n], pp_r.at[n], sib)
     sums = mm(wt[...], tokh[h])
     for n in range(5):
         pown[n] = sums[:, n * 128 : n * 128 + 128]
@@ -180,7 +188,7 @@
     cst[0, 0] = mc
     cst[0, 1] = l0 * g0 + pst[1] * g1
     for p in CHIP_FAR:
-        send(cst.at[0], cst.at[cid(p)], cst_s.at[cid(p)], cst_r.at[cid(p)], chip_dev(p))
+        send("pp", cst.at[0], cst.at[cid(p)], cst_s.at[cid(p)], cst_r.at[cid(p)], chip_dev(p))
     scale0 = jnp.broadcast_to(g0[0:1, :], (128, 128)).T
     scale1 = jnp.broadcast_to(g1[0:1, :], (128, 128)).T
 
@@ -193,11 +201,13 @@
         arrived(precv.at[pl.ds(n, w)], pp_s.at[n], pp_r.at[n])
         for q in range(n, n + w):
             pown[q] = pown[q] * scale0 + precv[q] * scale1
-    older = len(live)
     for p in CHIP_FAR:
         for n in range(5):
             rs_send[cid(p), :, pl.ds(n * 128, 128)] = unit(pown.at[n], chip_at(p)).astype(BF)
-        send(rs_send.at[cid(p)], rs_recv.at[cid(p)], rs_s.at[cid(p)], rs_r.at[cid(p)], chip_dev(p))
+        send("rs", rs_send.at[cid(p)], rs_recv.at[cid(p)], rs_s.at[cid(p)], rs_r.at[cid(p)], chip_dev(p))
+    theirs = pl.ds(pl.multiple_of(o * HALF, 128), HALF)
+    send("w", up_hbm.at[:, :, theirs], upv.at[:, units], w_s.at[0], w_r.at[0], sib)
+    send("w", dn_hbm.at[:, :, theirs], dnv.at[:, units], w_s.at[1], w_r.at[1], sib)
     yown = jnp.concatenate([unit(pown.at[n], chip) for n in range(5)], axis=1)
 
     for n in range(4):
@@ -215,7 +225,7 @@
             rows.append(mxs[n, pl.ds(8 * (1 - x_hi) + k, NZ, stride=16), :])
         mw[part, :] = jnp.concatenate(rows, axis=0).T.astype(BF)
 
-    drain(older)
+    drain(("tab",))
 
     for p in CHIP_NEAR:
         arrived(cst.at[cid(p)], cst_s.at[cid(p)], cst_r.at[cid(p)])
@@ -239,89 +249,75 @@
         arrived(rs_recv.at[j], rs_s.at[j], rs_r.at[j])
         acc += rs_recv[j].astype(F32) * fk[:, j : j + 1]
 
-    def rows_across(value, rows, recv, ssem, rsem):
-        older = len(live)
+    def rows_across(group, value, rows, recv, ssem, rsem, idle):
         rows[...] = value.reshape(NE, 1, HALF)
         for i in EXP_FAR:
             src = rows.at[i[0] * NZ + lax.rem(z + i[1], NZ)]
-            send(src, recv.at[i[0] * NZ + z], ssem.at[eid(i)], rsem.at[eid(i)], exp_dev(i))
+            send(group, src, recv.at[i[0] * NZ + z], ssem.at[eid(i)], rsem.at[eid(i)], exp_dev(i))
         recv[z] = rows[z]
-        drain(older)
+        drain(idle)
         for i in EXP_NEAR:
             dst = recv.at[i[0] * NZ + lax.rem(z + NZ - i[1], NZ)]
             arrived(dst, ssem.at[eid(i)], rsem.at[eid(i)])
         return recv[...].reshape(NE, HALF)
 
-    def spread(value, buf, gs, gr):
-        older = len(live)
-        buf[h, chip] = value
-        for p in CHIP_FAR:
-            send(buf.at[h, chip], buf.at[h, chip], gs.at[cid(p)], gr.at[cid(p)], chip_dev(p))
-        drain(older)
-
-    def forward(q, buf, gs, gr, fs, fr):
-        for p in ((q, 1), (q, 0)) if q else ((q, 1),):
-            arrived(buf.at[h, chip_from(p)], gs.at[cid(p)], gr.at[cid(p)])
-        src = buf.at[h, pl.ds(lax.rem(y + 4 - q, 4) * 2, 2)]
-        send(src, src, fs.at[q], fr.at[q], sib)
-
-    def other_half(q, buf, fs, fr):
-        arrived(buf.at[o, pl.ds(lax.rem(y + 4 - q, 4) * 2, 2)], fs.at[q], fr.at[q])
-
-    across = rows_across(acc, a_send, a_recv, a_s, a_r)
-    spread(across.astype(BF), xb, xg_s, xg_r)
+    across = rows_across("a", acc, a_send, a_recv, a_s, a_r, ("pp",))
+    xb[chip] = across.astype(BF)
+    for p in CHIP_FAR:
+        send("xg", xb.at[chip], xb.at[chip], xg_s.at[cid(p)], xg_r.at[cid(p)], chip_dev(p))
     for c in loads[4:]:
         c.wait()
-
-    def experts(q):
-        ks = (chip_from((q, 0)), chip_from((q, 1)))
-        other_half(q, xb, xf_s, xf_r)
-        inner = [nt(xb[0, k], upv[0, k]) + nt(xb[1, k], upv[1, k]) for k in ks]
-        hidden = [gelu(v).astype(BF) for v in inner]
-        away = [mm(v, dnv[o, k]) for v, k in zip(hidden, ks)]
+    arrived(upv.at[:, their_units], w_s.at[0], w_r.at[0])
+    arrived(dnv.at[:, their_units], w_s.at[1], w_r.at[1])
+
+    def first(q):
+        for p in ((q, 1), (q, 0)) if q else ((q, 1),):
+            arrived(xb.at[chip_from(p)], xg_s.at[cid(p)], xg_r.at[cid(p)])
         for n in range(2):
-            po_send[q, n] = away[n]
-        send(po_send.at[q], po_recv.at[q], po_s.at[q], po_r.at[q], sib)
-        here = [mm(v, dnv[h, k]) for v, k in zip(hidden, ks)]
+            k = chip_from((q, n))
+            px_send[q, n, :, pl.ds(0, 2 * FD)] = nt(xb[k], upv[k])
+        send("px", px_send.at[q], px_recv.at[q], px_s.at[q], px_r.at[q], sib)
+
+    def second(q):
+        arrived(px_recv.at[q], px_s.at[q], px_r.at[q])
+        both = []
         for n in range(2):
-            po_own[q, n] = here[n]
-
-    def reduce_on(q):
-        arrived(po_recv.at[q], po_s.at[q], po_r.at[q])
-        both = [po_own[q, n] + po_recv[q, n] for n in range(2)]
+            k = chip_from((q, n))
+            inner = px_send[q, n, :, pl.ds(0, 2 * FD)] + px_recv[q, n, :, pl.ds(0, 2 * FD)]
+            both.append(mm(gelu(inner).astype(BF), dnv[k]))
         for n in range(2):
             value = jnp.concatenate([both[n][:NZ], both[1 - n][NZ:]], axis=0)
             if q or n:
                 ro_send[q, n] = value.astype(BF)
                 p = (4 - q if q else 0, n)
                 sems = ro_s.at[cid(p)], ro_r.at[cid(p)]
-                send(ro_send.at[q, n], ro_recv.at[cid(p)], *sems, chip_dev(p))
+                send("ro", ro_send.at[q, n], ro_recv.at[cid(p)], *sems, chip_dev(p))
             else:
-                po_own[0, 0] = value
-
-    forward(0, xb, xg_s, xg_r, xf_s, xf_r)
-    forward(1, xb, xg_s, xg_r, xf_s, xf_r)
-    forward(3, xb, xg_s, xg_r, xf_s, xf_r)
-    experts(0)
-    experts(1)
-    forward(2, xb, xg_s, xg_r, xf_s, xf_r)
-    reduce_on(0)
-    experts(3)
-    reduce_on(1)
-    experts(2)
-    older = len(live)
-    reduce_on(3)
-    reduce_on(2)
-    acc = po_own[0, 0]
-    drain(older)
+                ro_own[...] = value
+
+    first(0)
+    first(1)
+    first(3)
+    second(0)
+    first(2)
+    second(1)
+    second(3)
+    second(2)
+    acc = ro_own[...]
+    drain(("rs", "a", "xg"))
     for p in CHIP_NEAR:
         arrived(ro_recv.at[cid(p)], ro_s.at[cid(p)], ro_r.at[cid(p)])
         acc += ro_recv[cid(p)].astype(F32)
 
-    across = rows_across(acc, b_send, b_recv, b_s, b_r)
-    spread(across.astype(BF), ret, rg_s, rg_r)
-    for q in (0, 1, 3, 2):
-        forward(q, ret, rg_s, rg_r, rf_s, rf_r)
+    across = rows_across("b", acc, b_send, b_recv, b_s, b_r, ("px", "w"))
+    ret[h, chip] = across.astype(BF)
+    for p in CHIP_FAR:
+        send("rg", ret.at[h, chip], ret.at[h, chip], rg_s.at[cid(p)], rg_r.at[cid(p)], chip_dev(p))
+        send("rg", ret.at[h, chip], ret.at[h, chip], rf_s.at[cid(p)], rf_r.at[cid(p)], (chip_at(p) * 2 + o, e))
+    send("rg", ret.at[h, chip], ret.at[h, chip], rf_s.at[0], rf_r.at[0], sib)
+    drain(("ro", "b"))
+    for p in CHIP_NEAR:
+        arrived(ret.at[h, chip_from(p)], rg_s.at[cid(p)], rg_r.at[cid(p)])
 
     def mix(half):
         table = ret[half].reshape(SLOTS, HALF)
@@ -331,8 +327,8 @@
             out_ref[part, lanes] = mm(mw[part, :], table).astype(BF)
 
     mix(h)
-    for q in (0, 1, 3, 2):
-        other_half(q, ret, rf_s, rf_r)
+    for p in ((0, 0),) + CHIP_NEAR:
+        arrived(ret.at[o, chip_from(p)], rf_s.at[cid(p)], rf_r.at[cid(p)])
     mix(o)
     drain()
 
@@ -347,8 +343,8 @@
         out_specs=pl.BlockSpec(memory_space=pltpu.VMEM),
         scratch_shapes=[
             vm((2, ROWS, HALF), BF),
-            vm((2, K, FD, HALF), BF),
-            vm((2, K, FD, HALF), BF),
+            vm((K, 2 * FD, HALF), BF),
+            vm((K, 2 * FD, HALF), BF),
             vm((2, NE, K, HALF), BF),
             vm((SLOTS, ROWS), F32),
             vm((SLOTS, ROWS), BF),
@@ -365,11 +361,11 @@
             vm((NC, NE, HALF), BF),
             vm((NE, 1, HALF), F32),
             vm((NE, 1, HALF), F32),
-            vm((2, NC, NE, HALF), BF),
-            vm((4, 2, NE, HALF), F32),
-            vm((4, 2, NE, HALF), F32),
-            vm((4, 2, NE, HALF), F32),
+            vm((NC, NE, HALF), BF),
+            vm((4, 2, NE, 384), F32),
+            vm((4, 2, NE, 384), F32),
             vm((4, 2, NE, HALF), BF),
+            vm((NE, HALF), F32),
             vm((NC, NE, HALF), BF),
             vm((NE, 1, HALF), F32),
             vm((NE, 1, HALF), F32),
@@ -382,12 +378,13 @@
             dma((NC,)), dma((NC,)),
             dma((5,)), dma((5,)),
             dma((NC,)), dma((NC,)),
+            dma((2,)), dma((2,)),
             dma((NE,)), dma((NE,)),
-            dma((NC,)), dma((NC,)), dma((4,)), dma((4,)),
+            dma((NC,)), dma((NC,)),
             dma((4,)), dma((4,)),
             dma((NC,)), dma((NC,)),
             dma((NE,)), dma((NE,)),
-            dma((NC,)), dma((NC,)), dma((4,)), dma((4,)),
+            dma((NC,)), dma((NC,)), dma((NC,)), dma((NC,)),
         ],
         compiler_params=pltpu.CompilerParams(
             collective_id=0, has_side_effects=True, vmem_limit_bytes=50 * 2**20
@@ -395,12 +392,8 @@
         cost_estimate=pl.CostEstimate(flops=1_400_000_000, bytes_accessed=14_000_000, transcendentals=400_000),
         name="soft_moe",
     )
-    mixed = call(
-        tokens.reshape(ROWS, 2 * HALF),
-        slot_params.T,
-        jnp.transpose(up_weight, (0, 2, 1)),
-        down_weight,
-    )
+    operands = (tokens.reshape(ROWS, 2 * HALF), slot_params.T, jnp.transpose(up_weight, (0, 2, 1)), down_weight)
+    mixed = call(*(pltpu.with_memory_space_constraint(v, pltpu.HBM) for v in operands))
     return mixed.reshape(tokens.shape)
 
 

time: 59.1 us -> 56.2 us (0.951)
  Pallas kernels: 56.7 us -> 54.6 us
  local copies, waits for them, and re-layouts: 2.22 us -> 1.49 us
    pallas_call x1, Pallas kernels: 56.7 us -> 54.6 us  [shards(): call(*(pltpu.with_memory_space_constraint(v, pltpu.HBM) for v in operands))]
    unnamed x3 -> x1, local copies, waits for them, and re-layouts: 2.22 us -> 1.49 us
where the time goes in v3:
time: 56.2 us; the launch traced here: 56.1 us
  Pallas kernels  54.6 us (97%)
  local copies, waits for them, and re-layouts  1.49 us (3%)
    pallas_call x1, Pallas kernels, shards(): call(*(pltpu.with_memory_space_constraint(v, pltpu.HBM) for v in operands))  54.6 us
    unnamed x1, local copies, waits for them, and re-layouts  1.49 us

profile of v3, /device:TPU:1, one launch (start us, length us, event | category | flops | bytes accessed | tf_op | source)
XLA Modules:
  0.0 56.1 jit_solution(2283175891189542038)
XLA Ops:
  0.0 54.6 %soft_moe.1 = bf16[1024,1280]{1,0:T(8,128)(2,1)S(1)} custom-call(bf16[1024,1280]{1,0:T(8,128)(2,1)} %bitcast.6, bf16[8,1280]{1,0:T(8,128)(2,1)} %bitcast.7, bf16[8,160,1280]{2,1,0:T(8,128)(2,1)} %bitcast.5, bf16[8,160,1280]{2,1,0:T(8,128)(2,1)} %dn_hbm.1), custom_call_target="tpu_custom_call" | custom-call | flops 1400000000 | bytes 14000000 | tf_op jit(solution)/shard_map/soft_moe/pallas_call | solution.py:396
  54.6 1.5 %copy.6 = bf16[1,1024,1280]{2,1,0:T(8,128)(2,1)} copy(bf16[1,1024,1280]{2,1,0:T(8,128)(2,1)S(1)} %bitcast.4) | data formatting | bytes 5242880

commit v4 on v3

--- a/solution.py
+++ b/solution.py
@@ -1,3 +1,5 @@
+import functools
+
 import jax
 import jax.numpy as jnp
 from jax import lax
@@ -16,6 +18,7 @@
 ROWS = 1024
 FD = 160
 SLOTS = NE * K
+PADDED = SLOTS + 16
 
 EXP_FAR = (
     (1, 4), (1, 3), (1, 5), (0, 4), (1, 2), (1, 6), (0, 3), (0, 5),
@@ -45,7 +48,7 @@
     px_send, px_recv, ro_send, ro_own, ro_recv, b_send, b_recv, ret, mxs, mw,
     load_sem, tab_s, tab_r, tabf_s, tabf_r, pst_s, pst_r, cst_s, cst_r, pp_s, pp_r,
     rs_s, rs_r, w_s, w_r, a_s, a_r, xg_s, xg_r, px_s, px_r, ro_s, ro_r, b_s, b_r,
-    rg_s, rg_r, rf_s, rf_r,
+    rg_s, rg_r,
 ):
     s = lax.axis_index("seq")
     e = lax.axis_index("expert")
@@ -71,9 +74,6 @@
     def exp_at(i):
         return lax.rem(z + i[1], NZ) * 2 + (1 - x_hi if i[0] else x_hi)
 
-    def exp_from(i):
-        return exp_at((i[0], NZ - i[1]))
-
     def exp_dev(i):
         return ((flipped if i[0] else chip) * 2 + h, exp_at(i))
 
@@ -82,6 +82,12 @@
 
     def eid(i):
         return i[0] * NZ + i[1]
+
+    def place_to(i):
+        return i[0] * NZ + (i[1] + 1) % NZ
+
+    def place_from(i):
+        return i[0] * NZ + (1 - i[1]) % NZ
 
     live = []
 
@@ -116,7 +122,7 @@
     loads = []
     for half in range(2):
         lanes = pl.ds(half * HALF, HALF)
-        c = pltpu.make_async_copy(sp_hbm.at[:, lanes], tab.at[half, e], load_sem.at[4 + half])
+        c = pltpu.make_async_copy(sp_hbm.at[:, lanes], tab.at[half, 1], load_sem.at[4 + half])
         c.start()
         loads.append(c)
     for half in range(2):
@@ -137,9 +143,9 @@
     pl.semaphore_wait(barrier, NE - 1 + 2 * (NC - 1) + 1)
 
     for i in EXP_FAR:
-        send("tab", tab.at[h, e], tab.at[h, e], tab_s.at[eid(i)], tab_r.at[eid(i)], exp_dev(i))
+        send("tab", tab.at[h, 1], tab.at[h, place_from(i)], tab_s.at[eid(i)], tab_r.at[eid(i)], exp_dev(i))
     for i in EXP_NEAR:
-        src = tab.at[h, exp_from(i)]
+        src = tab.at[h, place_from(i)]
         arrived(src, tab_s.at[eid(i)], tab_r.at[eid(i)])
         send("tab", src, src, tabf_s.at[eid(i)], tabf_r.at[eid(i)], sib)
     loads[2].wait()
@@ -149,7 +155,7 @@
         part = pl.ds(n * 256, 256)
         lg[:, part] = nt(half_table, tokh[h, part, :])
     for i in EXP_NEAR:
-        arrived(tab.at[o, exp_from(i)], tabf_s.at[eid(i)], tabf_r.at[eid(i)])
+        arrived(tab.at[o, place_from(i)], tabf_s.at[eid(i)], tabf_r.at[eid(i)])
     half_table = tab[o].astype(F32).reshape(SLOTS, HALF).astype(BF)
     for n in range(4):
         part = pl.ds(n * 256, 256)
@@ -178,8 +184,9 @@
         part = pl.ds(n, w)
         send("pp", psend.at[part], precv.at[part], pp_s.at[n], pp_r.at[n], sib)
     sums = mm(wt[...], tokh[h])
+    all_rows = pl.ds(0, SLOTS)
     for n in range(5):
-        pown[n] = sums[:, n * 128 : n * 128 + 128]
+        pown[n, all_rows, :] = sums[:, n * 128 : n * 128 + 128]
     arrived(pst, pst_s, pst_r)
     m1 = pst[0]
     mc = jnp.maximum(m0, m1)
@@ -193,14 +200,14 @@
     scale1 = jnp.broadcast_to(g1[0:1, :], (128, 128)).T
 
     def unit(ref, k):
-        near = ref[pl.ds(8 * x_hi + k, NZ, stride=16), :]
-        far = ref[pl.ds(8 * (1 - x_hi) + k + 1 - 2 * lax.rem(k, 2), NZ, stride=16), :]
+        near = ref[pl.ds(k, NZ, stride=K), :]
+        far = ref[pl.ds(NZ * K + k + 1 - 2 * lax.rem(k, 2), NZ, stride=K), :]
         return jnp.concatenate([near, far], axis=0)
 
     for n, w in ((0, 2), (2, 2), (4, 1)):
         arrived(precv.at[pl.ds(n, w)], pp_s.at[n], pp_r.at[n])
         for q in range(n, n + w):
-            pown[q] = pown[q] * scale0 + precv[q] * scale1
+            pown[q, all_rows, :] = pown[q, all_rows, :] * scale0 + precv[q] * scale1
     for p in CHIP_FAR:
         for n in range(5):
             rs_send[cid(p), :, pl.ds(n * 128, 128)] = unit(pown.at[n], chip_at(p)).astype(BF)
@@ -215,14 +222,15 @@
         v = lg[:, part]
         ex = jnp.exp(v - jnp.max(v, axis=0, keepdims=True))
         ex = ex / jnp.sum(ex, axis=0, keepdims=True)
-        mxs[2 * n] = ex[:, :128]
-        mxs[2 * n + 1] = ex[:, 128:]
+        mxs[2 * n, all_rows, :] = ex[:, :128]
+        mxs[2 * n + 1, all_rows, :] = ex[:, 128:]
     for n in range(8):
         part = pl.ds(n * 128, 128)
         rows = []
         for k in range(K):
-            rows.append(mxs[n, pl.ds(8 * x_hi + k, NZ, stride=16), :])
-            rows.append(mxs[n, pl.ds(8 * (1 - x_hi) + k, NZ, stride=16), :])
+            near = mxs[n, pl.ds(k, NZ, stride=K), :]
+            far = mxs[n, pl.ds(NZ * K + k, NZ, stride=K), :]
+            rows += [near[:4], far[:4], near[4:], far[4:]]
         mw[part, :] = jnp.concatenate(rows, axis=0).T.astype(BF)
 
     drain(("tab",))
@@ -240,7 +248,7 @@
     for j in range(NC):
         factors = jnp.where(row == j, jnp.exp(cst[j, 0] - top) / total, factors)
     fin[0:8, :] = factors
-    ft[...] = fin[...].T
+    ft[all_rows, :] = fin[...].T
     fk = unit(ft, chip)
 
     acc = yown * fk[:, 0:1]
@@ -249,88 +257,145 @@
         arrived(rs_recv.at[j], rs_s.at[j], rs_r.at[j])
         acc += rs_recv[j].astype(F32) * fk[:, j : j + 1]
 
-    def rows_across(group, value, rows, recv, ssem, rsem, idle):
-        rows[...] = value.reshape(NE, 1, HALF)
-        for i in EXP_FAR:
-            src = rows.at[i[0] * NZ + lax.rem(z + i[1], NZ)]
-            send(group, src, recv.at[i[0] * NZ + z], ssem.at[eid(i)], rsem.at[eid(i)], exp_dev(i))
-        recv[z] = rows[z]
-        drain(idle)
-        for i in EXP_NEAR:
-            dst = recv.at[i[0] * NZ + lax.rem(z + NZ - i[1], NZ)]
-            arrived(dst, ssem.at[eid(i)], rsem.at[eid(i)])
-        return recv[...].reshape(NE, HALF)
-
-    across = rows_across("a", acc, a_send, a_recv, a_s, a_r, ("pp",))
-    xb[chip] = across.astype(BF)
-    for p in CHIP_FAR:
-        send("xg", xb.at[chip], xb.at[chip], xg_s.at[cid(p)], xg_r.at[cid(p)], chip_dev(p))
+    batch = lax.div(z, 4)
+    place = batch * 8 + lax.rem(z, 4)
+    a_send[...] = acc.reshape(NE, 1, HALF)
+    for i in EXP_FAR:
+        src = a_send.at[place_to(i)]
+        there = place + 4 * i[0]
+        send("a", src, a_recv.at[there], a_s.at[eid(i)], a_r.at[there], exp_dev(i))
+    a_recv[place] = a_send[1]
+    drain(("pp",))
     for c in loads[4:]:
         c.wait()
     arrived(upv.at[:, their_units], w_s.at[0], w_r.at[0])
     arrived(dnv.at[:, their_units], w_s.at[1], w_r.at[1])
 
-    def first(q):
+    def rows_in(b):
+        for n in range(8):
+            wait = functools.partial(arrived, a_recv.at[b * 8 + n], a_s.at[0], a_r.at[b * 8 + n])
+            if n < 4:
+                pl.when(z != b * 4 + n)(wait)
+            else:
+                wait()
+        xb[chip, b] = a_recv[pl.ds(b * 8, 8)].reshape(8, HALF).astype(BF)
+        for p in CHIP_FAR:
+            send("xg", xb.at[chip, b], xb.at[chip, b], xg_s.at[b, cid(p)], xg_r.at[b, cid(p)], chip_dev(p))
+
+    def first(b, q):
         for p in ((q, 1), (q, 0)) if q else ((q, 1),):
-            arrived(xb.at[chip_from(p)], xg_s.at[cid(p)], xg_r.at[cid(p)])
+            arrived(xb.at[chip_from(p), b], xg_s.at[b, cid(p)], xg_r.at[b, cid(p)])
         for n in range(2):
             k = chip_from((q, n))
-            px_send[q, n, :, pl.ds(0, 2 * FD)] = nt(xb[k], upv[k])
-        send("px", px_send.at[q], px_recv.at[q], px_s.at[q], px_r.at[q], sib)
-
-    def second(q):
-        arrived(px_recv.at[q], px_s.at[q], px_r.at[q])
+            px_send[b, q, n, :, pl.ds(0, 2 * FD)] = nt(xb[k, b], upv[k])
+        send("px", px_send.at[b, q], px_recv.at[b, q], px_s.at[b, q], px_r.at[b, q], sib)
+
+    row8 = lax.broadcasted_iota(jnp.int32, (8, HALF), 0)
+
+    def second(b, q):
+        arrived(px_recv.at[b, q], px_s.at[b, q], px_r.at[b, q])
         both = []
         for n in range(2):
             k = chip_from((q, n))
-            inner = px_send[q, n, :, pl.ds(0, 2 * FD)] + px_recv[q, n, :, pl.ds(0, 2 * FD)]
+            inner = px_send[b, q, n, :, pl.ds(0, 2 * FD)] + px_recv[b, q, n, :, pl.ds(0, 2 * FD)]
             both.append(mm(gelu(inner).astype(BF), dnv[k]))
         for n in range(2):
-            value = jnp.concatenate([both[n][:NZ], both[1 - n][NZ:]], axis=0)
+            value = jnp.where(row8 < 4, both[n], both[1 - n])
             if q or n:
-                ro_send[q, n] = value.astype(BF)
+                ro_send[b, q, n] = value.astype(BF)
                 p = (4 - q if q else 0, n)
-                sems = ro_s.at[cid(p)], ro_r.at[cid(p)]
-                send("ro", ro_send.at[q, n], ro_recv.at[cid(p)], *sems, chip_dev(p))
+                sems = ro_s.at[b, cid(p)], ro_r.at[b, cid(p)]
+                send("ro", ro_send.at[b, q, n], ro_recv.at[b, cid(p)], *sems, chip_dev(p))
             else:
-                ro_own[...] = value
-
-    first(0)
-    first(1)
-    first(3)
-    second(0)
-    first(2)
-    second(1)
-    second(3)
-    second(2)
-    acc = ro_own[...]
-    drain(("rs", "a", "xg"))
-    for p in CHIP_NEAR:
-        arrived(ro_recv.at[cid(p)], ro_s.at[cid(p)], ro_r.at[cid(p)])
-        acc += ro_recv[cid(p)].astype(F32)
-
-    across = rows_across("b", acc, b_send, b_recv, b_s, b_r, ("px", "w"))
-    ret[h, chip] = across.astype(BF)
-    for p in CHIP_FAR:
-        send("rg", ret.at[h, chip], ret.at[h, chip], rg_s.at[cid(p)], rg_r.at[cid(p)], chip_dev(p))
-        send("rg", ret.at[h, chip], ret.at[h, chip], rf_s.at[cid(p)], rf_r.at[cid(p)], (chip_at(p) * 2 + o, e))
-    send("rg", ret.at[h, chip], ret.at[h, chip], rf_s.at[0], rf_r.at[0], sib)
-    drain(("ro", "b"))
-    for p in CHIP_NEAR:
-        arrived(ret.at[h, chip_from(p)], rg_s.at[cid(p)], rg_r.at[cid(p)])
+                ro_own[b] = value
+
+    def rows_out(b):
+        total_b = ro_own[b]
+        for p in CHIP_NEAR:
+            arrived(ro_recv.at[b, cid(p)], ro_s.at[b, cid(p)], ro_r.at[b, cid(p)])
+            total_b += ro_recv[b, cid(p)].astype(F32)
+        b_send[pl.ds(b * 8, 8)] = total_b.reshape(8, 1, HALF)
+        for turn in range(4):
+            for rel in (1, 0):
+                to_z = b * 4 + turn
+                src = b_send.at[b * 8 + rel * 4 + turn]
+                dev = ((flipped if rel else chip) * 2 + h, to_z * 2 + (1 - x_hi if rel else x_hi))
+                u = lax.rem(z - to_z + 9, NZ)
+                there = lax.div(u, 4) * 8 + rel * 4 + lax.rem(u, 4)
+                c = copy(src, b_recv.at[there], b_s.at[b, rel * 4 + turn], b_r.at[there], dev)
+                if rel:
+                    c.start()
+                else:
+                    pl.when(z != to_z)(c.start)
+        here = b * 8 + lax.rem(z, 4)
+
+        @pl.when(batch == b)
+        def _():
+            b_recv[1] = b_send[here]
+
+    def rows_out_done(b):
+        for turn in range(4):
+            for rel in range(2):
+                c = copy(b_send.at[0], b_recv.at[0], b_s.at[b, rel * 4 + turn], b_r.at[0], sib)
+                if rel:
+                    c.wait_send()
+                else:
+                    pl.when(z != b * 4 + turn)(c.wait_send)
+
+    def result_copies(g):
+        mine = ret.at[h, chip, g]
+        for target in [c * 2 + core for c in range(NC) for core in (1, 0)]:
+            yield copy(mine, mine, rg_s.at[g, target], rg_r.at[g, h, chip], (target, e)), target
+
+    def results(g):
+        for c, target in result_copies(g):
+            pl.when(target != s)(c.start)
+
+    def own_clip(g):
+        for j in range(g * 8, g * 8 + 8):
+            if j != 1:
+                arrived(b_recv.at[j], b_s.at[0, 0], b_r.at[j])
+        ret[h, chip, g] = b_recv[pl.ds(g * 8, 8)].reshape(8, HALF).astype(BF)
+        results(g)
+
+    rows_in(0)
+    rows_in(1)
+    for q in (0, 1, 3, 2):
+        first(0, q)
+    for q in (0, 1, 3, 2):
+        second(0, q)
+    for q in (0, 1, 3, 2):
+        first(1, q)
+    for q in (0, 1, 3, 2):
+        second(1, q)
+    drain(("rs", "a", "w", "xg"))
+    rows_out(0)
+    rows_out(1)
+    own_clip(0)
+    own_clip(1)
+    drain(("px", "ro"))
+    rows_out_done(0)
+    rows_out_done(1)
+    for g in range(2):
+        for p in CHIP_NEAR:
+            arrived(ret.at[h, chip_from(p), g], rg_s.at[g, 0], rg_r.at[g, h, chip_from(p)])
 
     def mix(half):
-        table = ret[half].reshape(SLOTS, HALF)
+        table = ret[half].astype(F32).reshape(SLOTS, HALF).astype(BF)
         lanes = pl.ds(pl.multiple_of(half * HALF, 128), HALF)
         for n in range(4):
             part = pl.ds(n * 256, 256)
             out_ref[part, lanes] = mm(mw[part, :], table).astype(BF)
 
     mix(h)
-    for p in ((0, 0),) + CHIP_NEAR:
-        arrived(ret.at[o, chip_from(p)], rf_s.at[cid(p)], rf_r.at[cid(p)])
+    for g in range(2):
+        for p in ((0, 0),) + CHIP_NEAR:
+            arrived(ret.at[o, chip_from(p), g], rg_s.at[g, 0], rg_r.at[g, o, chip_from(p)])
     mix(o)
     drain()
+    for g in range(2):
+        for c, target in result_copies(g):
+            pl.when(target != s)(c.wait_send)
 
 
 def shards(tokens, slot_params, up_weight, down_weight):
@@ -353,24 +418,24 @@
             vm((2, 8, 128), F32),
             vm((NC, 2, 8, 128), F32),
             vm((128, 128), F32),
-            vm((128, 128), F32),
+            vm((PADDED, 128), F32),
             vm((5, SLOTS, 128), F32),
-            vm((5, SLOTS, 128), F32),
+            vm((5, PADDED, 128), F32),
             vm((5, SLOTS, 128), F32),
             vm((NC, NE, HALF), BF),
             vm((NC, NE, HALF), BF),
             vm((NE, 1, HALF), F32),
             vm((NE, 1, HALF), F32),
-            vm((NC, NE, HALF), BF),
-            vm((4, 2, NE, 384), F32),
-            vm((4, 2, NE, 384), F32),
-            vm((4, 2, NE, HALF), BF),
-            vm((NE, HALF), F32),
-            vm((NC, NE, HALF), BF),
+            vm((NC, 2, 8, HALF), BF),
+            vm((2, 4, 2, 8, 384), F32),
+            vm((2, 4, 2, 8, 384), F32),
+            vm((2, 4, 2, 8, HALF), BF),
+            vm((2, 8, HALF), F32),
+            vm((2, NC, 8, HALF), BF),
             vm((NE, 1, HALF), F32),
             vm((NE, 1, HALF), F32),
-            vm((2, NC, NE, HALF), BF),
-            vm((8, SLOTS, 128), F32),
+            vm((2, NC, 2, 8, HALF), BF),
+            vm((8, PADDED, 128), F32),
             vm((ROWS, SLOTS), BF),
             dma((8,)),
             dma((NE,)), dma((NE,)), dma((NE,)), dma((NE,)),
@@ -380,11 +445,11 @@
             dma((NC,)), dma((NC,)),
             dma((2,)), dma((2,)),
             dma((NE,)), dma((NE,)),
-            dma((NC,)), dma((NC,)),
-            dma((4,)), dma((4,)),
-            dma((NC,)), dma((NC,)),
-            dma((NE,)), dma((NE,)),
-            dma((NC,)), dma((NC,)), dma((NC,)), dma((NC,)),
+            dma((2, NC)), dma((2, NC)),
+            dma((2, 4)), dma((2, 4)),
+            dma((2, NC)), dma((2, NC)),
+            dma((2, 8)), dma((NE,)),
+            dma((2, 2 * NC)), dma((2, 2, NC)),
         ],
         compiler_params=pltpu.CompilerParams(
             collective_id=0, has_side_effects=True, vmem_limit_bytes=50 * 2**20

time: 56.2 us -> 54.9 us (0.977)
  Pallas kernels: 54.6 us -> 53.3 us
    pallas_call x1, Pallas kernels: 54.6 us -> 53.3 us  [shards(): call(*(pltpu.with_memory_space_constraint(v, pltpu.HBM) for v in operands))]
where the time goes in v4:
time: 54.9 us; the launch traced here: 54.8 us
  Pallas kernels  53.3 us (97%)
  local copies, waits for them, and re-layouts  1.49 us (3%)
    pallas_call x1, Pallas kernels, shards(): call(*(pltpu.with_memory_space_constraint(v, pltpu.HBM) for v in operands))  53.3 us
    unnamed x1, local copies, waits for them, and re-layouts  1.49 us

profile of v4, /device:TPU:1, one launch (start us, length us, event | category | flops | bytes accessed | tf_op | source)
XLA Modules:
  0.0 54.8 jit_solution(764481395228826235)
XLA Ops:
  0.0 53.3 %soft_moe.1 = bf16[1024,1280]{1,0:T(8,128)(2,1)S(1)} custom-call(bf16[1024,1280]{1,0:T(8,128)(2,1)} %bitcast.6, bf16[8,1280]{1,0:T(8,128)(2,1)} %bitcast.7, bf16[8,160,1280]{2,1,0:T(8,128)(2,1)} %bitcast.5, bf16[8,160,1280]{2,1,0:T(8,128)(2,1)} %dn_hbm.1), custom_call_target="tpu_custom_call" | custom-call | flops 1400000000 | bytes 14000000 | tf_op jit(solution)/shard_map/soft_moe/pallas_call | solution.py:461
  53.3 1.5 %copy.6 = bf16[1,1024,1280]{2,1,0:T(8,128)(2,1)} copy(bf16[1,1024,1280]{2,1,0:T(8,128)(2,1)S(1)} %bitcast.4) | data formatting | bytes 5242880

commit v5 on v4

--- a/solution.py
+++ b/solution.py
@@ -82,9 +82,6 @@
 
     def eid(i):
         return i[0] * NZ + i[1]
-
-    def place_to(i):
-        return i[0] * NZ + (i[1] + 1) % NZ
 
     def place_from(i):
         return i[0] * NZ + (1 - i[1]) % NZ
@@ -147,15 +144,14 @@
     for i in EXP_NEAR:
         src = tab.at[h, place_from(i)]
         arrived(src, tab_s.at[eid(i)], tab_r.at[eid(i)])
-        send("tab", src, src, tabf_s.at[eid(i)], tabf_r.at[eid(i)], sib)
+        send("tab", src, src, tabf_s.at[eid(i)], tabf_r, sib)
     loads[2].wait()
     loads[3].wait()
     half_table = tab[h].astype(F32).reshape(SLOTS, HALF).astype(BF)
     for n in range(4):
         part = pl.ds(n * 256, 256)
         lg[:, part] = nt(half_table, tokh[h, part, :])
-    for i in EXP_NEAR:
-        arrived(tab.at[o, place_from(i)], tabf_s.at[eid(i)], tabf_r.at[eid(i)])
+    arrived(tab.at[o, pl.ds(0, NE - 1)], tabf_s.at[0], tabf_r)
     half_table = tab[o].astype(F32).reshape(SLOTS, HALF).astype(BF)
     for n in range(4):
         part = pl.ds(n * 256, 256)
@@ -195,14 +191,18 @@
     cst[0, 0] = mc
     cst[0, 1] = l0 * g0 + pst[1] * g1
     for p in CHIP_FAR:
-        send("pp", cst.at[0], cst.at[cid(p)], cst_s.at[cid(p)], cst_r.at[cid(p)], chip_dev(p))
+        send("pp", cst.at[0], cst.at[cid(p)], cst_s.at[cid(p)], cst_r, chip_dev(p))
     scale0 = jnp.broadcast_to(g0[0:1, :], (128, 128)).T
     scale1 = jnp.broadcast_to(g1[0:1, :], (128, 128)).T
 
     def unit(ref, k):
         near = ref[pl.ds(k, NZ, stride=K), :]
         far = ref[pl.ds(NZ * K + k + 1 - 2 * lax.rem(k, 2), NZ, stride=K), :]
-        return jnp.concatenate([near, far], axis=0)
+        return jnp.concatenate([near[:4], far[:4], near[4:], far[4:]], axis=0)
+
+    def sums_to(g, p):
+        j = cid(p)
+        send("rs", rs_send.at[g, j], rs_recv.at[g, j], rs_s.at[g, j], rs_r.at[g], chip_dev(p))
 
     for n, w in ((0, 2), (2, 2), (4, 1)):
         arrived(precv.at[pl.ds(n, w)], pp_s.at[n], pp_r.at[n])
@@ -210,8 +210,12 @@
             pown[q, all_rows, :] = pown[q, all_rows, :] * scale0 + precv[q] * scale1
     for p in CHIP_FAR:
         for n in range(5):
-            rs_send[cid(p), :, pl.ds(n * 128, 128)] = unit(pown.at[n], chip_at(p)).astype(BF)
-        send("rs", rs_send.at[cid(p)], rs_recv.at[cid(p)], rs_s.at[cid(p)], rs_r.at[cid(p)], chip_dev(p))
+            rows = unit(pown.at[n], chip_at(p))
+            for g in range(2):
+                rs_send[g, cid(p), :, pl.ds(n * 128, 128)] = rows[g * 8 : g * 8 + 8].astype(BF)
+        sums_to(1, p)
+    for p in CHIP_FAR:
+        sums_to(0, p)
     theirs = pl.ds(pl.multiple_of(o * HALF, 128), HALF)
     send("w", up_hbm.at[:, :, theirs], upv.at[:, units], w_s.at[0], w_r.at[0], sib)
     send("w", dn_hbm.at[:, :, theirs], dnv.at[:, units], w_s.at[1], w_r.at[1], sib)
@@ -235,8 +239,7 @@
 
     drain(("tab",))
 
-    for p in CHIP_NEAR:
-        arrived(cst.at[cid(p)], cst_s.at[cid(p)], cst_r.at[cid(p)])
+    arrived(cst.at[pl.ds(1, NC - 1)], cst_s.at[0], cst_r)
     top = cst[0, 0]
     for j in range(1, NC):
         top = jnp.maximum(top, cst[j, 0])
@@ -251,19 +254,21 @@
     ft[all_rows, :] = fin[...].T
     fk = unit(ft, chip)
 
-    acc = yown * fk[:, 0:1]
-    for p in CHIP_NEAR:
-        j = cid(p)
-        arrived(rs_recv.at[j], rs_s.at[j], rs_r.at[j])
-        acc += rs_recv[j].astype(F32) * fk[:, j : j + 1]
-
     batch = lax.div(z, 4)
     place = batch * 8 + lax.rem(z, 4)
-    a_send[...] = acc.reshape(NE, 1, HALF)
-    for i in EXP_FAR:
-        src = a_send.at[place_to(i)]
-        there = place + 4 * i[0]
-        send("a", src, a_recv.at[there], a_s.at[eid(i)], a_r.at[there], exp_dev(i))
+    for g in (1, 0):
+        rows = slice(g * 8, g * 8 + 8)
+        acc = yown[rows] * fk[rows, 0:1]
+        arrived(rs_recv.at[g, pl.ds(1, NC - 1)], rs_s.at[g, 0], rs_r.at[g])
+        for j in range(1, NC):
+            acc += rs_recv[g, j].astype(F32) * fk[rows, j : j + 1]
+        a_send[pl.ds(g * 8, 8)] = acc.reshape(8, 1, HALF)
+        for i in EXP_FAR:
+            u = (i[1] + 1) % NZ
+            if u // 4 == g:
+                src = a_send.at[g * 8 + i[0] * 4 + u % 4]
+                there = place + 4 * i[0]
+                send("a", src, a_recv.at[there], a_s.at[eid(i)], a_r.at[batch], exp_dev(i))
     a_recv[place] = a_send[1]
     drain(("pp",))
     for c in loads[4:]:
@@ -272,12 +277,9 @@
     arrived(dnv.at[:, their_units], w_s.at[1], w_r.at[1])
 
     def rows_in(b):
-        for n in range(8):
-            wait = functools.partial(arrived, a_recv.at[b * 8 + n], a_s.at[0], a_r.at[b * 8 + n])
-            if n < 4:
-                pl.when(z != b * 4 + n)(wait)
-            else:
-                wait()
+        for others, here in ((7, batch == b), (8, batch != b)):
+            wait = functools.partial(arrived, a_recv.at[pl.ds(b * 8, others)], a_s.at[0], a_r.at[b])
+            pl.when(here)(wait)
         xb[chip, b] = a_recv[pl.ds(b * 8, 8)].reshape(8, HALF).astype(BF)
         for p in CHIP_FAR:
             send("xg", xb.at[chip, b], xb.at[chip, b], xg_s.at[b, cid(p)], xg_r.at[b, cid(p)], chip_dev(p))
@@ -304,16 +306,16 @@
             if q or n:
                 ro_send[b, q, n] = value.astype(BF)
                 p = (4 - q if q else 0, n)
-                sems = ro_s.at[b, cid(p)], ro_r.at[b, cid(p)]
+                sems = ro_s.at[b, cid(p)], ro_r.at[b]
                 send("ro", ro_send.at[b, q, n], ro_recv.at[b, cid(p)], *sems, chip_dev(p))
             else:
                 ro_own[b] = value
 
     def rows_out(b):
         total_b = ro_own[b]
-        for p in CHIP_NEAR:
-            arrived(ro_recv.at[b, cid(p)], ro_s.at[b, cid(p)], ro_r.at[b, cid(p)])
-            total_b += ro_recv[b, cid(p)].astype(F32)
+        arrived(ro_recv.at[b, pl.ds(1, NC - 1)], ro_s.at[b, 0], ro_r.at[b])
+        for j in range(1, NC):
+            total_b += ro_recv[b, j].astype(F32)
         b_send[pl.ds(b * 8, 8)] = total_b.reshape(8, 1, HALF)
         for turn in range(4):
             for rel in (1, 0):
@@ -322,7 +324,7 @@
                 dev = ((flipped if rel else chip) * 2 + h, to_z * 2 + (1 - x_hi if rel else x_hi))
                 u = lax.rem(z - to_z + 9, NZ)
                 there = lax.div(u, 4) * 8 + rel * 4 + lax.rem(u, 4)
-                c = copy(src, b_recv.at[there], b_s.at[b, rel * 4 + turn], b_r.at[there], dev)
+                c = copy(src, b_recv.at[there], b_s.at[b, rel * 4 + turn], b_r.at[lax.div(u, 4)], dev)
                 if rel:
                     c.start()
                 else:
@@ -345,16 +347,14 @@
     def result_copies(g):
         mine = ret.at[h, chip, g]
         for target in [c * 2 + core for c in range(NC) for core in (1, 0)]:
-            yield copy(mine, mine, rg_s.at[g, target], rg_r.at[g, h, chip], (target, e)), target
+            yield copy(mine, mine, rg_s.at[g], rg_r.at[g, h], (target, e)), target
 
     def results(g):
         for c, target in result_copies(g):
             pl.when(target != s)(c.start)
 
     def own_clip(g):
-        for j in range(g * 8, g * 8 + 8):
-            if j != 1:
-                arrived(b_recv.at[j], b_s.at[0, 0], b_r.at[j])
+        arrived(b_recv.at[pl.ds(g * 8, 7 + g)], b_s.at[0, 0], b_r.at[g])
         ret[h, chip, g] = b_recv[pl.ds(g * 8, 8)].reshape(8, HALF).astype(BF)
         results(g)
 
@@ -377,8 +377,7 @@
     rows_out_done(0)
     rows_out_done(1)
     for g in range(2):
-        for p in CHIP_NEAR:
-            arrived(ret.at[h, chip_from(p), g], rg_s.at[g, 0], rg_r.at[g, h, chip_from(p)])
+        arrived(tab.at[0, pl.ds(0, NC - 1)], rg_s.at[g], rg_r.at[g, h])
 
     def mix(half):
         table = ret[half].astype(F32).reshape(SLOTS, HALF).astype(BF)
@@ -389,13 +388,12 @@
 
     mix(h)
     for g in range(2):
-        for p in ((0, 0),) + CHIP_NEAR:
-            arrived(ret.at[o, chip_from(p), g], rg_s.at[g, 0], rg_r.at[g, o, chip_from(p)])
+        arrived(tab.at[0, pl.ds(0, NC)], rg_s.at[g], rg_r.at[g, o])
     mix(o)
     drain()
     for g in range(2):
-        for c, target in result_copies(g):
-            pl.when(target != s)(c.wait_send)
+        block = tab.at[0, pl.ds(0, 2 * NC - 1)]
+        copy(block, block, rg_s.at[g], rg_r.at[g, 0], sib).wait_send()
 
 
 def shards(tokens, slot_params, up_weight, down_weight):
@@ -422,8 +420,8 @@
             vm((5, SLOTS, 128), F32),
             vm((5, PADDED, 128), F32),
             vm((5, SLOTS, 128), F32),
-            vm((NC, NE, HALF), BF),
-            vm((NC, NE, HALF), BF),
+            vm((2, NC, 8, HALF), BF),
+            vm((2, NC, 8, HALF), BF),
             vm((NE, 1, HALF), F32),
             vm((NE, 1, HALF), F32),
             vm((NC, 2, 8, HALF), BF),
@@ -438,18 +436,18 @@
             vm((8, PADDED, 128), F32),
             vm((ROWS, SLOTS), BF),
             dma((8,)),
-            dma((NE,)), dma((NE,)), dma((NE,)), dma((NE,)),
+            dma((NE,)), dma((NE,)), dma((NE,)), dma,
             dma, dma,
-            dma((NC,)), dma((NC,)),
+            dma((NC,)), dma,
             dma((5,)), dma((5,)),
-            dma((NC,)), dma((NC,)),
+            dma((2, NC)), dma((2,)),
             dma((2,)), dma((2,)),
-            dma((NE,)), dma((NE,)),
+            dma((NE,)), dma((2,)),
             dma((2, NC)), dma((2, NC)),
             dma((2, 4)), dma((2, 4)),
-            dma((2, NC)), dma((2, NC)),
-            dma((2, 8)), dma((NE,)),
-            dma((2, 2 * NC)), dma((2, 2, NC)),
+            dma((2, NC)), dma((2,)),
+            dma((2, 8)), dma((2,)),
+            dma((2,)), dma((2, 2)),
         ],
         compiler_params=pltpu.CompilerParams(
             collective_id=0, has_side_effects=True, vmem_limit_bytes=50 * 2**20

time: 54.9 us -> 53.1 us (0.967)
  Pallas kernels: 53.3 us -> 51.4 us
    pallas_call x1, Pallas kernels: 53.3 us -> 51.4 us  [shards(): call(*(pltpu.with_memory_space_constraint(v, pltpu.HBM) for v in operands))]
where the time goes in v5:
time: 53.1 us; the launch traced here: 52.9 us
  Pallas kernels  51.4 us (97%)
  local copies, waits for them, and re-layouts  1.49 us (3%)
    pallas_call x1, Pallas kernels, shards(): call(*(pltpu.with_memory_space_constraint(v, pltpu.HBM) for v in operands))  51.4 us
    unnamed x1, local copies, waits for them, and re-layouts  1.49 us

profile of v5, /device:TPU:1, one launch (start us, length us, event | category | flops | bytes accessed | tf_op | source)
XLA Modules:
  0.0 52.9 jit_solution(10106026391496607133)
XLA Ops:
  0.0 51.4 %soft_moe.1 = bf16[1024,1280]{1,0:T(8,128)(2,1)S(1)} custom-call(bf16[1024,1280]{1,0:T(8,128)(2,1)} %bitcast.6, bf16[8,1280]{1,0:T(8,128)(2,1)} %bitcast.7, bf16[8,160,1280]{2,1,0:T(8,128)(2,1)} %bitcast.5, bf16[8,160,1280]{2,1,0:T(8,128)(2,1)} %dn_hbm.1), custom_call_target="tpu_custom_call" | custom-call | flops 1400000000 | bytes 14000000 | tf_op jit(solution)/shard_map/soft_moe/pallas_call | solution.py:459
  51.5 1.5 %copy.6 = bf16[1,1024,1280]{2,1,0:T(8,128)(2,1)} copy(bf16[1,1024,1280]{2,1,0:T(8,128)(2,1)S(1)} %bitcast.4) | data formatting | bytes 5242880

commit v6 on v5

--- a/solution.py
+++ b/solution.py
@@ -86,23 +86,19 @@
     def place_from(i):
         return i[0] * NZ + (1 - i[1]) % NZ
 
-    live = []
-
-    def drain(groups=None):
-        for item in list(live):
-            if groups is None or item[0] in groups:
-                item[1].wait_send()
-                live.remove(item)
-
     def copy(src, dst, ssem, rsem, dev):
         return pltpu.make_async_remote_copy(
             src_ref=src, dst_ref=dst, send_sem=ssem, recv_sem=rsem, device_id=dev, device_id_type=MESH
         )
 
-    def send(group, src, dst, ssem, rsem, dev):
-        c = copy(src, dst, ssem, rsem, dev)
-        c.start()
-        live.append((group, c))
+    def send(src, dst, ssem, rsem, dev):
+        copy(src, dst, ssem, rsem, dev).start()
+
+    def sent(ref, ssem):
+        copy(ref, ref, ssem, ssem, sib).wait_send()
+
+    def blocks(n):
+        return tab.at[0, pl.ds(0, n)]
 
     def arrived(dst, ssem, rsem):
         copy(dst, dst, ssem, rsem, sib).wait_recv()
@@ -117,16 +113,14 @@
     pl.semaphore_signal(barrier, inc=1, device_id=sib, device_id_type=MESH)
 
     loads = []
-    for half in range(2):
-        lanes = pl.ds(half * HALF, HALF)
-        c = pltpu.make_async_copy(sp_hbm.at[:, lanes], tab.at[half, 1], load_sem.at[4 + half])
-        c.start()
-        loads.append(c)
+    ours = pl.ds(pl.multiple_of(h * HALF, 128), HALF)
+    c = pltpu.make_async_copy(sp_hbm.at[:, ours], tab.at[h, 1], load_sem.at[4])
+    c.start()
+    loads.append(c)
     for half in range(2):
         c = pltpu.make_async_copy(tok_hbm.at[:, pl.ds(half * HALF, HALF)], tokh.at[half], load_sem.at[half])
         c.start()
         loads.append(c)
-    ours = pl.ds(pl.multiple_of(h * HALF, 128), HALF)
     units = pl.ds(pl.multiple_of(h * FD, 16), FD)
     their_units = pl.ds(pl.multiple_of(o * FD, 16), FD)
     for n, (src, dst) in enumerate(((up_hbm, upv), (dn_hbm, dnv))):
@@ -136,22 +130,21 @@
     fin[...] = jnp.zeros_like(fin)
     px_send[...] = jnp.zeros_like(px_send)
     loads[0].wait()
+    pl.semaphore_wait(barrier, NE - 1 + 2 * (NC - 1) + 1)
+
+    for i in EXP_FAR:
+        send(tab.at[h, 1], tab.at[h, place_from(i)], tab_s, tab_r.at[place_from(i) // 4], exp_dev(i))
+    for g in (0, 2, 1, 3):
+        arrived(blocks(4 if g else 3), tab_s, tab_r.at[g])
+        four = tab.at[h, pl.ds(4 * g, 4)]
+        send(four, four, tabf_s, tabf_r, sib)
     loads[1].wait()
-    pl.semaphore_wait(barrier, NE - 1 + 2 * (NC - 1) + 1)
-
-    for i in EXP_FAR:
-        send("tab", tab.at[h, 1], tab.at[h, place_from(i)], tab_s.at[eid(i)], tab_r.at[eid(i)], exp_dev(i))
-    for i in EXP_NEAR:
-        src = tab.at[h, place_from(i)]
-        arrived(src, tab_s.at[eid(i)], tab_r.at[eid(i)])
-        send("tab", src, src, tabf_s.at[eid(i)], tabf_r, sib)
     loads[2].wait()
-    loads[3].wait()
     half_table = tab[h].astype(F32).reshape(SLOTS, HALF).astype(BF)
     for n in range(4):
         part = pl.ds(n * 256, 256)
         lg[:, part] = nt(half_table, tokh[h, part, :])
-    arrived(tab.at[o, pl.ds(0, NE - 1)], tabf_s.at[0], tabf_r)
+    arrived(tab.at[o], tabf_s, tabf_r)
     half_table = tab[o].astype(F32).reshape(SLOTS, HALF).astype(BF)
     for n in range(4):
         part = pl.ds(n * 256, 256)
@@ -171,14 +164,14 @@
     l0 = jnp.broadcast_to(xt[64:65, :], (8, 128))
     stat[0] = m0
     stat[1] = l0
-    send("tab", stat, pst, pst_s, pst_r, sib)
+    send(stat, pst, pst_s, pst_r, sib)
 
     for n, w in ((0, 2), (2, 2), (4, 1)):
         sums = mm(wt[...], tokh[o, :, pl.ds(n * 128, w * 128)])
         for q in range(w):
             psend[n + q] = sums[:, q * 128 : q * 128 + 128]
         part = pl.ds(n, w)
-        send("pp", psend.at[part], precv.at[part], pp_s.at[n], pp_r.at[n], sib)
+        send(psend.at[part], precv.at[part], pp_s, pp_r.at[n], sib)
     sums = mm(wt[...], tokh[h])
     all_rows = pl.ds(0, SLOTS)
     for n in range(5):
@@ -191,7 +184,7 @@
     cst[0, 0] = mc
     cst[0, 1] = l0 * g0 + pst[1] * g1
     for p in CHIP_FAR:
-        send("pp", cst.at[0], cst.at[cid(p)], cst_s.at[cid(p)], cst_r, chip_dev(p))
+        send(cst.at[0], cst.at[cid(p)], cst_s, cst_r, chip_dev(p))
     scale0 = jnp.broadcast_to(g0[0:1, :], (128, 128)).T
     scale1 = jnp.broadcast_to(g1[0:1, :], (128, 128)).T
 
@@ -202,10 +195,10 @@
 
     def sums_to(g, p):
         j = cid(p)
-        send("rs", rs_send.at[g, j], rs_recv.at[g, j], rs_s.at[g, j], rs_r.at[g], chip_dev(p))
+        send(rs_send.at[g, j], rs_recv.at[g, j], rs_s, rs_r.at[g], chip_dev(p))
 
     for n, w in ((0, 2), (2, 2), (4, 1)):
-        arrived(precv.at[pl.ds(n, w)], pp_s.at[n], pp_r.at[n])
+        arrived(precv.at[pl.ds(n, w)], pp_s, pp_r.at[n])
         for q in range(n, n + w):
             pown[q, all_rows, :] = pown[q, all_rows, :] * scale0 + precv[q] * scale1
     for p in CHIP_FAR:
@@ -217,8 +210,8 @@
     for p in CHIP_FAR:
         sums_to(0, p)
     theirs = pl.ds(pl.multiple_of(o * HALF, 128), HALF)
-    send("w", up_hbm.at[:, :, theirs], upv.at[:, units], w_s.at[0], w_r.at[0], sib)
-    send("w", dn_hbm.at[:, :, theirs], dnv.at[:, units], w_s.at[1], w_r.at[1], sib)
+    send(up_hbm.at[:, :, theirs], upv.at[:, units], w_s.at[0], w_r.at[0], sib)
+    send(dn_hbm.at[:, :, theirs], dnv.at[:, units], w_s.at[1], w_r.at[1], sib)
     yown = jnp.concatenate([unit(pown.at[n], chip) for n in range(5)], axis=1)
 
     for n in range(4):
@@ -237,9 +230,11 @@
             rows += [near[:4], far[:4], near[4:], far[4:]]
         mw[part, :] = jnp.concatenate(rows, axis=0).T.astype(BF)
 
-    drain(("tab",))
-
-    arrived(cst.at[pl.ds(1, NC - 1)], cst_s.at[0], cst_r)
+    sent(blocks(NE - 1), tab_s)
+    sent(tab.at[h], tabf_s)
+    sent(stat, pst_s)
+
+    arrived(cst.at[pl.ds(1, NC - 1)], cst_s, cst_r)
     top = cst[0, 0]
     for j in range(1, NC):
         top = jnp.maximum(top, cst[j, 0])
@@ -259,7 +254,7 @@
     for g in (1, 0):
         rows = slice(g * 8, g * 8 + 8)
         acc = yown[rows] * fk[rows, 0:1]
-        arrived(rs_recv.at[g, pl.ds(1, NC - 1)], rs_s.at[g, 0], rs_r.at[g])
+        arrived(rs_recv.at[g, pl.ds(1, NC - 1)], rs_s, rs_r.at[g])
         for j in range(1, NC):
             acc += rs_recv[g, j].astype(F32) * fk[rows, j : j + 1]
         a_send[pl.ds(g * 8, 8)] = acc.reshape(8, 1, HALF)
@@ -268,34 +263,34 @@
             if u // 4 == g:
                 src = a_send.at[g * 8 + i[0] * 4 + u % 4]
                 there = place + 4 * i[0]
-                send("a", src, a_recv.at[there], a_s.at[eid(i)], a_r.at[batch], exp_dev(i))
+                send(src, a_recv.at[there], a_s, a_r.at[batch], exp_dev(i))
     a_recv[place] = a_send[1]
-    drain(("pp",))
-    for c in loads[4:]:
+    sent(psend, pp_s)
+    sent(cst.at[pl.ds(1, NC - 1)], cst_s)
+    for c in loads[3:]:
         c.wait()
     arrived(upv.at[:, their_units], w_s.at[0], w_r.at[0])
     arrived(dnv.at[:, their_units], w_s.at[1], w_r.at[1])
 
     def rows_in(b):
         for others, here in ((7, batch == b), (8, batch != b)):
-            wait = functools.partial(arrived, a_recv.at[pl.ds(b * 8, others)], a_s.at[0], a_r.at[b])
+            wait = functools.partial(arrived, a_recv.at[pl.ds(b * 8, others)], a_s, a_r.at[b])
             pl.when(here)(wait)
         xb[chip, b] = a_recv[pl.ds(b * 8, 8)].reshape(8, HALF).astype(BF)
         for p in CHIP_FAR:
-            send("xg", xb.at[chip, b], xb.at[chip, b], xg_s.at[b, cid(p)], xg_r.at[b, cid(p)], chip_dev(p))
+            send(xb.at[chip, b], xb.at[chip, b], xg_s, xg_r.at[b, p[0]], chip_dev(p))
 
     def first(b, q):
-        for p in ((q, 1), (q, 0)) if q else ((q, 1),):
-            arrived(xb.at[chip_from(p), b], xg_s.at[b, cid(p)], xg_r.at[b, cid(p)])
+        arrived(blocks(2 if q else 1), xg_s, xg_r.at[b, q])
         for n in range(2):
             k = chip_from((q, n))
             px_send[b, q, n, :, pl.ds(0, 2 * FD)] = nt(xb[k, b], upv[k])
-        send("px", px_send.at[b, q], px_recv.at[b, q], px_s.at[b, q], px_r.at[b, q], sib)
+        send(px_send.at[b, q], px_recv.at[b, q], px_s, px_r.at[b, q], sib)
 
     row8 = lax.broadcasted_iota(jnp.int32, (8, HALF), 0)
 
     def second(b, q):
-        arrived(px_recv.at[b, q], px_s.at[b, q], px_r.at[b, q])
+        arrived(px_recv.at[b, q], px_s, px_r.at[b, q])
         both = []
         for n in range(2):
             k = chip_from((q, n))
@@ -306,14 +301,14 @@
             if q or n:
                 ro_send[b, q, n] = value.astype(BF)
                 p = (4 - q if q else 0, n)
-                sems = ro_s.at[b, cid(p)], ro_r.at[b]
-                send("ro", ro_send.at[b, q, n], ro_recv.at[b, cid(p)], *sems, chip_dev(p))
+                sems = ro_s, ro_r.at[b]
+                send(ro_send.at[b, q, n], ro_recv.at[b, cid(p)], *sems, chip_dev(p))
             else:
                 ro_own[b] = value
 
     def rows_out(b):
         total_b = ro_own[b]
-        arrived(ro_recv.at[b, pl.ds(1, NC - 1)], ro_s.at[b, 0], ro_r.at[b])
+        arrived(ro_recv.at[b, pl.ds(1, NC - 1)], ro_s, ro_r.at[b])
         for j in range(1, NC):
             total_b += ro_recv[b, j].astype(F32)
         b_send[pl.ds(b * 8, 8)] = total_b.reshape(8, 1, HALF)
@@ -324,7 +319,7 @@
                 dev = ((flipped if rel else chip) * 2 + h, to_z * 2 + (1 - x_hi if rel else x_hi))
                 u = lax.rem(z - to_z + 9, NZ)
                 there = lax.div(u, 4) * 8 + rel * 4 + lax.rem(u, 4)
-                c = copy(src, b_recv.at[there], b_s.at[b, rel * 4 + turn], b_r.at[lax.div(u, 4)], dev)
+                c = copy(src, b_recv.at[there], b_s, b_r.at[lax.div(u, 4)], dev)
                 if rel:
                     c.start()
                 else:
@@ -335,15 +330,6 @@
         def _():
             b_recv[1] = b_send[here]
 
-    def rows_out_done(b):
-        for turn in range(4):
-            for rel in range(2):
-                c = copy(b_send.at[0], b_recv.at[0], b_s.at[b, rel * 4 + turn], b_r.at[0], sib)
-                if rel:
-                    c.wait_send()
-                else:
-                    pl.when(z != b * 4 + turn)(c.wait_send)
-
     def result_copies(g):
         mine = ret.at[h, chip, g]
         for target in [c * 2 + core for c in range(NC) for core in (1, 0)]:
@@ -354,7 +340,7 @@
             pl.when(target != s)(c.start)
 
     def own_clip(g):
-        arrived(b_recv.at[pl.ds(g * 8, 7 + g)], b_s.at[0, 0], b_r.at[g])
+        arrived(b_recv.at[pl.ds(g * 8, 7 + g)], b_s, b_r.at[g])
         ret[h, chip, g] = b_recv[pl.ds(g * 8, 8)].reshape(8, HALF).astype(BF)
         results(g)
 
@@ -368,16 +354,20 @@
         first(1, q)
     for q in (0, 1, 3, 2):
         second(1, q)
-    drain(("rs", "a", "w", "xg"))
+    sent(blocks(2 * NC - 2), rs_s)
+    sent(a_recv.at[pl.ds(0, NE - 1)], a_s)
+    sent(blocks(2 * NC - 2), xg_s)
+    sent(upv.at[:, units], w_s.at[0])
+    sent(dnv.at[:, units], w_s.at[1])
     rows_out(0)
     rows_out(1)
     own_clip(0)
     own_clip(1)
-    drain(("px", "ro"))
-    rows_out_done(0)
-    rows_out_done(1)
+    sent(px_send, px_s)
+    sent(blocks(2 * NC - 2), ro_s)
+    sent(b_recv.at[pl.ds(0, NE - 1)], b_s)
     for g in range(2):
-        arrived(tab.at[0, pl.ds(0, NC - 1)], rg_s.at[g], rg_r.at[g, h])
+        arrived(blocks(NC - 1), rg_s.at[g], rg_r.at[g, h])
 
     def mix(half):
         table = ret[half].astype(F32).reshape(SLOTS, HALF).astype(BF)
@@ -388,12 +378,10 @@
 
     mix(h)
     for g in range(2):
-        arrived(tab.at[0, pl.ds(0, NC)], rg_s.at[g], rg_r.at[g, o])
+        arrived(blocks(NC), rg_s.at[g], rg_r.at[g, o])
     mix(o)
-    drain()
     for g in range(2):
-        block = tab.at[0, pl.ds(0, 2 * NC - 1)]
-        copy(block, block, rg_s.at[g], rg_r.at[g, 0], sib).wait_send()
+        sent(blocks(2 * NC - 1), rg_s.at[g])
 
 
 def shards(tokens, slot_params, up_weight, down_weight):
@@ -436,17 +424,17 @@
             vm((8, PADDED, 128), F32),
             vm((ROWS, SLOTS), BF),
             dma((8,)),
-            dma((NE,)), dma((NE,)), dma((NE,)), dma,
+            dma, dma((4,)), dma, dma,
             dma, dma,
-            dma((NC,)), dma,
-            dma((5,)), dma((5,)),
-            dma((2, NC)), dma((2,)),
+            dma, dma,
+            dma, dma((5,)),
+            dma, dma((2,)),
             dma((2,)), dma((2,)),
-            dma((NE,)), dma((2,)),
-            dma((2, NC)), dma((2, NC)),
-            dma((2, 4)), dma((2, 4)),
-            dma((2, NC)), dma((2,)),
-            dma((2, 8)), dma((2,)),
+            dma, dma((2,)),
+            dma, dma((2, 4)),
+            dma, dma((2, 4)),
+            dma, dma((2,)),
+            dma, dma((2,)),
             dma((2,)), dma((2, 2)),
         ],
         compiler_params=pltpu.CompilerParams(

time: 53.1 us -> 51.8 us (0.976)
  Pallas kernels: 51.4 us -> 50.2 us
    pallas_call x1, Pallas kernels: 51.4 us -> 50.2 us  [shards(): call(*(pltpu.with_memory_space_constraint(v, pltpu.HBM) for v in operands))]
where the time goes in v6:
time: 51.8 us; the launch traced here: 51.7 us
  Pallas kernels  50.2 us (97%)
  local copies, waits for them, and re-layouts  1.49 us (3%)
    pallas_call x1, Pallas kernels, shards(): call(*(pltpu.with_memory_space_constraint(v, pltpu.HBM) for v in operands))  50.2 us
    unnamed x1, local copies, waits for them, and re-layouts  1.49 us

profile of v6, /device:TPU:1, one launch (start us, length us, event | category | flops | bytes accessed | tf_op | source)
XLA Modules:
  0.0 51.7 jit_solution(7480687846599250223)
XLA Ops:
  0.0 50.2 %soft_moe.1 = bf16[1024,1280]{1,0:T(8,128)(2,1)S(1)} custom-call(bf16[1024,1280]{1,0:T(8,128)(2,1)} %bitcast.6, bf16[8,1280]{1,0:T(8,128)(2,1)} %bitcast.7, bf16[8,160,1280]{2,1,0:T(8,128)(2,1)} %bitcast.5, bf16[8,160,1280]{2,1,0:T(8,128)(2,1)} %dn_hbm.1), custom_call_target="tpu_custom_call" | custom-call | flops 1400000000 | bytes 14000000 | tf_op jit(solution)/shard_map/soft_moe/pallas_call | solution.py:447
  50.2 1.5 %copy.6 = bf16[1,1024,1280]{2,1,0:T(8,128)(2,1)} copy(bf16[1,1024,1280]{2,1,0:T(8,128)(2,1)S(1)} %bitcast.4) | data formatting | bytes 5242880

commit v7 on v6

--- a/solution.py
+++ b/solution.py
@@ -354,15 +354,15 @@
         first(1, q)
     for q in (0, 1, 3, 2):
         second(1, q)
+    rows_out(0)
+    rows_out(1)
+    own_clip(0)
+    own_clip(1)
     sent(blocks(2 * NC - 2), rs_s)
     sent(a_recv.at[pl.ds(0, NE - 1)], a_s)
     sent(blocks(2 * NC - 2), xg_s)
     sent(upv.at[:, units], w_s.at[0])
     sent(dnv.at[:, units], w_s.at[1])
-    rows_out(0)
-    rows_out(1)
-    own_clip(0)
-    own_clip(1)
     sent(px_send, px_s)
     sent(blocks(2 * NC - 2), ro_s)
     sent(b_recv.at[pl.ds(0, NE - 1)], b_s)

time: 51.8 us -> 51.8 us (level)
  no operation moved by 1% of the time
where the time goes in v7:
time: 51.8 us; the launch traced here: 51.7 us
  Pallas kernels  50.2 us (97%)
  local copies, waits for them, and re-layouts  1.49 us (3%)
    pallas_call x1, Pallas kernels, shards(): call(*(pltpu.with_memory_space_constraint(v, pltpu.HBM) for v in operands))  50.2 us
    unnamed x1, local copies, waits for them, and re-layouts  1.49 us

profile of v7, /device:TPU:1, one launch (start us, length us, event | category | flops | bytes accessed | tf_op | source)
XLA Modules:
  0.0 51.7 jit_solution(6153372288837285042)
XLA Ops:
  0.0 50.2 %soft_moe.1 = bf16[1024,1280]{1,0:T(8,128)(2,1)S(1)} custom-call(bf16[1024,1280]{1,0:T(8,128)(2,1)} %bitcast.6, bf16[8,1280]{1,0:T(8,128)(2,1)} %bitcast.7, bf16[8,160,1280]{2,1,0:T(8,128)(2,1)} %bitcast.5, bf16[8,160,1280]{2,1,0:T(8,128)(2,1)} %dn_hbm.1), custom_call_target="tpu_custom_call" | custom-call | flops 1400000000 | bytes 14000000 | tf_op jit(solution)/shard_map/soft_moe/pallas_call | solution.py:447
  50.2 1.5 %copy.6 = bf16[1,1024,1280]{2,1,0:T(8,128)(2,1)} copy(bf16[1,1024,1280]{2,1,0:T(8,128)(2,1)S(1)} %bitcast.4) | data formatting | bytes 5242880
